TPU v7x, 256 devices: a whole 4x4x8 slice. The times are simulated.
256 devices in a mesh: shots: 16 (over z, core), gy: 4 (over y), gx: 4 (over x).
Axes of the slice: x: 4, y: 4, z: 8, core: 2. Of those that a mesh axis runs over, the one named last changes fastest.
Arguments:
- shot_cells: int32 [16, 4, 4, 16, 4096], P('shots', 'gy', 'gx'), may hold values from 0 to 8191
- shot_dose: float32 [16, 4, 4, 16, 4096], P('shots', 'gy', 'gx'), may hold values from 0.04 to 0.12
- shot_counts: int32 [16, 4, 4, 16], P('shots', 'gy', 'gx'), may hold values from 2048 to 4096, as said below
- materials: int32 [1024, 2048], P(('shots', 'gy'), 'gx'), may hold values from 0 to 3
- coefficients: float32 [4], replicated, may hold values from 0.04 to 0.24
- target: float32 [1024, 2048], P(('shots', 'gy'), 'gx'), may hold values from -6 to 6
Outputs:
- exposure: float32 [1024, 2048], P(('shots', 'gy'), 'gx')
- shot_grad: float32 [16, 4, 4, 16, 4096], P('shots', 'gy', 'gx')
Inputs may be any that keep to these rules, and one draw needn't show every extreme that they name: `shot_counts`: in every partition and tile some strip has all 4096 slots live; every count is at least 2048.
All inputs are finite; a program needn't handle non-finite values.
Results may differ from a plain program's by a relative error of at most 0.00007.
Values sent between devices are 32-bit elements; how exact they have to be, the bound alone decides.
No kernel may reach another device: no remote copies, remote signals or barrier semaphores. Data moves between devices by JAX's collectives and lax.ppermute only.
A program may use at most 64 MiB of HBM per device.

v0:
```python
import jax
import jax.numpy as jnp
from jax import lax
from jax.sharding import PartitionSpec as P

STEPS = 3


def extended(block, sides, width):
    for axis, dim in sides:
        count = lax.axis_size(axis)
        forward = [(i, i + 1) for i in range(count - 1)]
        backward = [(target, source) for source, target in forward]
        low = lax.ppermute(
            lax.slice_in_dim(block, block.shape[dim] - width, None, axis=dim), axis, forward
        )
        high = lax.ppermute(lax.slice_in_dim(block, 0, width, axis=dim), axis, backward)
        block = jnp.concatenate([low, block, high], axis=dim)
    return block


def one_hots(cells, rows, cols):
    row_ids = cells // cols
    col_ids = cells % cols
    row_table = (
        lax.broadcasted_iota(jnp.int32, (rows, cells.shape[0]), 0) == row_ids[None, :]
    ).astype(jnp.float32)
    col_table = (
        col_ids[:, None] == lax.broadcasted_iota(jnp.int32, (cells.shape[0], cols), 1)
    ).astype(jnp.float32)
    return (row_table, col_table)


def deposit_strip(cells, dose, rows, cols):
    row_table, col_table = one_hots(cells, rows, cols)
    return jnp.dot(
        row_table * dose[None, :],
        col_table,
        precision=lax.Precision.HIGHEST,
        preferred_element_type=jnp.float32,
    )


def pick_strip(cells, field):
    rows, cols = field.shape
    row_table, col_table = one_hots(cells, rows, cols)
    across = lax.dot_general(
        field,
        col_table,
        (((1,), (1,)), ((), ())),
        precision=lax.Precision.HIGHEST,
        preferred_element_type=jnp.float32,
    )
    return jnp.sum(across * row_table, axis=0)


def lookup(materials, coefficients):
    spread = jnp.zeros(materials.shape, jnp.float32)
    for index in range(coefficients.shape[0]):
        spread = spread + jnp.where(materials == index, coefficients[index], jnp.float32(0.0))
    return spread


def inner_sum(padded):
    return padded[2:, 1:-1] + padded[:-2, 1:-1] + padded[1:-1, 2:] + padded[1:-1, :-2]


def forward_blur(field, spread):
    for step in range(STEPS):
        padded = extended(field, ((("shots", "gy"), 0), ("gx", 1)), 1)
        field = field + spread * (inner_sum(padded) - 4.0 * field)
    return field


def adjoint_blur(field, spread):
    for step in range(STEPS):
        weighted = spread * field
        padded = extended(weighted, ((("shots", "gy"), 0), ("gx", 1)), 1)
        field = field + inner_sum(padded) - 4.0 * weighted
    return field


def local(shot_cells, shot_dose, shot_counts, materials, coefficients, target):
    cells = shot_cells[0, 0, 0]
    owners, slots = cells.shape
    rows, cols = materials.shape
    live = lax.broadcasted_iota(jnp.int32, (owners, slots), 1) < shot_counts[0, 0, 0][:, None]
    dose = jnp.where(live, shot_dose[0, 0, 0], jnp.float32(0.0))
    spread = lookup(materials, coefficients)
    partial_value = lax.map(lambda pair: deposit_strip(pair[0], pair[1], rows, cols), (cells, dose))
    dose_grid = lax.psum_scatter(partial_value, "shots", scatter_dimension=0, tiled=True)[0]
    exposure = forward_blur(dose_grid, spread)
    adjoint = adjoint_blur(exposure - target, spread)
    whole = lax.all_gather(adjoint, "shots", axis=0, tiled=True)
    strips = whole.reshape(owners, rows, cols)
    picked = lax.map(lambda pair: pick_strip(pair[0], pair[1]), (cells, strips))
    shot_grad = jnp.where(live, picked, jnp.float32(0.0))
    return (exposure, shot_grad[None, None, None])


def solution(mesh):
    placed = (
        P("shots", "gy", "gx", None, None),
        P("shots", "gy", "gx", None, None),
        P("shots", "gy", "gx", None),
        P(("shots", "gy"), "gx"),
        P(),
        P(("shots", "gy"), "gx"),
    )
    return jax.shard_map(
        local,
        mesh=mesh,
        in_specs=placed,
        out_specs=(P(("shots", "gy"), "gx"), P("shots", "gy", "gx", None, None)),
        check_vma=False,
    )
```

profile of v0, /device:TPU:5, one launch (start us, length us, event | category | flops | bytes accessed | tf_op | source)
XLA Modules:
  0.0 383.2 jit_solution(4620997328395946653)
XLA Ops:
  8.3 70.7 %while.26 = (s32[]{:T(128)}, f32[16,16,512]{2,1,0:T(8,128)}, s32[16,4096]{1,0:T(8,128)}, f32[16,4096]{1,0:T(8,128)S(1)}) while((s32[]{:T(128)}, f32[16,16,512]{2,1,0:T(8,128)}, s32[16,4096]{1,0:T(8,128)}, f32[16,4096]{1,0:T(8,128)S(1)}) %tuple.92), condition=%wide.region_1.2_spmd.clone, body=%wide.region_0.1_spmd.sunk.clone | while | flops 404987904 | bytes 197181 | solution.py:90
  79.0 56.7 %reduce-scatter.2.cloned.1.call-done = f32[1,16,512]{2,1,0:T(8,128)} async-done(((f32[16,16,512]{2,1,0:T(8,128)}), f32[1,16,512]{2,1,0:T(8,128)}) %reduce-scatter.2.cloned.1.call-update) | async-done | bytes 32784 | tf_op jit(solution)/shard_map/reduce_scatter | solution.py:91
  136.4 7.8 %collective-permute-start = (f32[1,512]{1,0:T(1,128)S(1)}, f32[1,512]{1,0:T(1,128)S(1)}, u32[]{:S(2)}, u32[]{:S(2)}) collective-permute-start(f32[1,512]{1,0:T(1,128)S(1)} %get-tuple-element.164), channel_id=1, source_target_pairs={{4,0},{8,4},{12,8},{16,12},{20,16},{24,20},{28,24},{32,28},{36,32}... | collective-permute-start | bytes 6152 | tf_op jit(solution)/shard_map/ppermute | solution.py:17
  166.9 4.2 %collective-permute-done.5 = f32[1,512]{1,0:T(1,128)S(1)} collective-permute-done((f32[1,512]{1,0:T(1,128)S(1)}, f32[1,512]{1,0:T(1,128)S(1)}, u32[]{:S(2)}, u32[]{:S(2)}) %collective-permute-start.5) | collective-permute-done | bytes 2080 | tf_op jit(solution)/shard_map/ppermute | solution.py:14
  185.6 4.2 %collective-permute-done.9 = f32[1,512]{1,0:T(1,128)S(1)} collective-permute-done((f32[1,512]{1,0:T(1,128)S(1)}, f32[1,512]{1,0:T(1,128)S(1)}, u32[]{:S(2)}, u32[]{:S(2)}) %collective-permute-start.9) | collective-permute-done | bytes 2080 | tf_op jit(solution)/shard_map/ppermute | solution.py:14
  204.7 3.9 %collective-permute-done.13 = f32[1,512]{1,0:T(1,128)S(1)} collective-permute-done((f32[1,512]{1,0:T(1,128)S(1)}, f32[1,512]{1,0:T(1,128)S(1)}, u32[]{:S(2)}, u32[]{:S(2)}) %collective-permute-start.13) | collective-permute-done | bytes 2080 | tf_op jit(solution)/shard_map/ppermute | solution.py:14
  251.7 29.6 %all_gather.3 = f32[256,512]{1,0:T(8,128)S(1)} all-gather(f32[16,512]{1,0:T(8,128)S(1)} %fusion.20), channel_id=1, replica_groups=mesh['shots'=16,'gy'=4,'gx'=4] {'shots'}, dimensions={0}, use_global_device_ids=true | all-gather | bytes 557056 | tf_op jit(solution)/shard_map/all_gather | solution.py:94
  281.4 94.2 %while.27 = (s32[]{:T(128)}, f32[16,4096]{1,0:T(8,128)S(1)}, s32[16,4096]{1,0:T(8,128)}, f32[16,16,512]{2,1,0:T(8,128)S(1)}) while((s32[]{:T(128)}, f32[16,4096]{1,0:T(8,128)S(1)}, s32[16,4096]{1,0:T(8,128)}, f32[16,16,512]{2,1,0:T(8,128)S(1)}) %tuple.93), condition=%wide.region_5.6_spmd.clone, body=%wide.region_3.5_spmd.sunk.clone | while | flops 405049344 | bytes 196673 | solution.py:96
  282.4 4.4 %fusion.73 = f32[4096]{0:T(1024)S(1)} fusion(s32[4096]{0:T(1024)S(1)} %add_select_fusion.7, s32[4096]{0:T(1024)S(1)} %bitcast.57, f32[16,16,512]{2,1,0:T(8,128)S(1)} %get-tuple-element.275, s32[]{:T(128)} %get-tuple-element.268), kind=kOutput, calls=%fused_computation.25.clone.1.clone | convolution fusion | flops 404942848 | bytes 81924 | tf_op jit(solution)/shard_map/while/body/eval_jaxpr/dot_general | solution.py:47
  288.3 4.4 %fusion.73 = f32[4096]{0:T(1024)S(1)} fusion(s32[4096]{0:T(1024)S(1)} %add_select_fusion.7, s32[4096]{0:T(1024)S(1)} %bitcast.57, f32[16,16,512]{2,1,0:T(8,128)S(1)} %get-tuple-element.275, s32[]{:T(128)} %get-tuple-element.268), kind=kOutput, calls=%fused_computation.25.clone.1.clone | convolution fusion | flops 404942848 | bytes 81924 | tf_op jit(solution)/shard_map/while/body/eval_jaxpr/dot_general | solution.py:47
  294.2 4.4 %fusion.73 = f32[4096]{0:T(1024)S(1)} fusion(s32[4096]{0:T(1024)S(1)} %add_select_fusion.7, s32[4096]{0:T(1024)S(1)} %bitcast.57, f32[16,16,512]{2,1,0:T(8,128)S(1)} %get-tuple-element.275, s32[]{:T(128)} %get-tuple-element.268), kind=kOutput, calls=%fused_computation.25.clone.1.clone | convolution fusion | flops 404942848 | bytes 81924 | tf_op jit(solution)/shard_map/while/body/eval_jaxpr/dot_general | solution.py:47
  300.1 4.4 %fusion.73 = f32[4096]{0:T(1024)S(1)} fusion(s32[4096]{0:T(1024)S(1)} %add_select_fusion.7, s32[4096]{0:T(1024)S(1)} %bitcast.57, f32[16,16,512]{2,1,0:T(8,128)S(1)} %get-tuple-element.275, s32[]{:T(128)} %get-tuple-element.268), kind=kOutput, calls=%fused_computation.25.clone.1.clone | convolution fusion | flops 404942848 | bytes 81924 | tf_op jit(solution)/shard_map/while/body/eval_jaxpr/dot_general | solution.py:47
  305.9 4.4 %fusion.73 = f32[4096]{0:T(1024)S(1)} fusion(s32[4096]{0:T(1024)S(1)} %add_select_fusion.7, s32[4096]{0:T(1024)S(1)} %bitcast.57, f32[16,16,512]{2,1,0:T(8,128)S(1)} %get-tuple-element.275, s32[]{:T(128)} %get-tuple-element.268), kind=kOutput, calls=%fused_computation.25.clone.1.clone | convolution fusion | flops 404942848 | bytes 81924 | tf_op jit(solution)/shard_map/while/body/eval_jaxpr/dot_general | solution.py:47
  311.8 4.4 %fusion.73 = f32[4096]{0:T(1024)S(1)} fusion(s32[4096]{0:T(1024)S(1)} %add_select_fusion.7, s32[4096]{0:T(1024)S(1)} %bitcast.57, f32[16,16,512]{2,1,0:T(8,128)S(1)} %get-tuple-element.275, s32[]{:T(128)} %get-tuple-element.268), kind=kOutput, calls=%fused_computation.25.clone.1.clone | convolution fusion | flops 404942848 | bytes 81924 | tf_op jit(solution)/shard_map/while/body/eval_jaxpr/dot_general | solution.py:47
  317.7 4.4 %fusion.73 = f32[4096]{0:T(1024)S(1)} fusion(s32[4096]{0:T(1024)S(1)} %add_select_fusion.7, s32[4096]{0:T(1024)S(1)} %bitcast.57, f32[16,16,512]{2,1,0:T(8,128)S(1)} %get-tuple-element.275, s32[]{:T(128)} %get-tuple-element.268), kind=kOutput, calls=%fused_computation.25.clone.1.clone | convolution fusion | flops 404942848 | bytes 81924 | tf_op jit(solution)/shard_map/while/body/eval_jaxpr/dot_general | solution.py:47
  323.6 4.4 %fusion.73 = f32[4096]{0:T(1024)S(1)} fusion(s32[4096]{0:T(1024)S(1)} %add_select_fusion.7, s32[4096]{0:T(1024)S(1)} %bitcast.57, f32[16,16,512]{2,1,0:T(8,128)S(1)} %get-tuple-element.275, s32[]{:T(128)} %get-tuple-element.268), kind=kOutput, calls=%fused_computation.25.clone.1.clone | convolution fusion | flops 404942848 | bytes 81924 | tf_op jit(solution)/shard_map/while/body/eval_jaxpr/dot_general | solution.py:47
  329.5 4.4 %fusion.73 = f32[4096]{0:T(1024)S(1)} fusion(s32[4096]{0:T(1024)S(1)} %add_select_fusion.7, s32[4096]{0:T(1024)S(1)} %bitcast.57, f32[16,16,512]{2,1,0:T(8,128)S(1)} %get-tuple-element.275, s32[]{:T(128)} %get-tuple-element.268), kind=kOutput, calls=%fused_computation.25.clone.1.clone | convolution fusion | flops 404942848 | bytes 81924 | tf_op jit(solution)/shard_map/while/body/eval_jaxpr/dot_general | solution.py:47
  335.4 4.4 %fusion.73 = f32[4096]{0:T(1024)S(1)} fusion(s32[4096]{0:T(1024)S(1)} %add_select_fusion.7, s32[4096]{0:T(1024)S(1)} %bitcast.57, f32[16,16,512]{2,1,0:T(8,128)S(1)} %get-tuple-element.275, s32[]{:T(128)} %get-tuple-element.268), kind=kOutput, calls=%fused_computation.25.clone.1.clone | convolution fusion | flops 404942848 | bytes 81924 | tf_op jit(solution)/shard_map/while/body/eval_jaxpr/dot_general | solution.py:47
  341.3 4.4 %fusion.73 = f32[4096]{0:T(1024)S(1)} fusion(s32[4096]{0:T(1024)S(1)} %add_select_fusion.7, s32[4096]{0:T(1024)S(1)} %bitcast.57, f32[16,16,512]{2,1,0:T(8,128)S(1)} %get-tuple-element.275, s32[]{:T(128)} %get-tuple-element.268), kind=kOutput, calls=%fused_computation.25.clone.1.clone | convolution fusion | flops 404942848 | bytes 81924 | tf_op jit(solution)/shard_map/while/body/eval_jaxpr/dot_general | solution.py:47
  347.2 4.4 %fusion.73 = f32[4096]{0:T(1024)S(1)} fusion(s32[4096]{0:T(1024)S(1)} %add_select_fusion.7, s32[4096]{0:T(1024)S(1)} %bitcast.57, f32[16,16,512]{2,1,0:T(8,128)S(1)} %get-tuple-element.275, s32[]{:T(128)} %get-tuple-element.268), kind=kOutput, calls=%fused_computation.25.clone.1.clone | convolution fusion | flops 404942848 | bytes 81924 | tf_op jit(solution)/shard_map/while/body/eval_jaxpr/dot_general | solution.py:47
  353.0 4.4 %fusion.73 = f32[4096]{0:T(1024)S(1)} fusion(s32[4096]{0:T(1024)S(1)} %add_select_fusion.7, s32[4096]{0:T(1024)S(1)} %bitcast.57, f32[16,16,512]{2,1,0:T(8,128)S(1)} %get-tuple-element.275, s32[]{:T(128)} %get-tuple-element.268), kind=kOutput, calls=%fused_computation.25.clone.1.clone | convolution fusion | flops 404942848 | bytes 81924 | tf_op jit(solution)/shard_map/while/body/eval_jaxpr/dot_general | solution.py:47
  358.9 4.4 %fusion.73 = f32[4096]{0:T(1024)S(1)} fusion(s32[4096]{0:T(1024)S(1)} %add_select_fusion.7, s32[4096]{0:T(1024)S(1)} %bitcast.57, f32[16,16,512]{2,1,0:T(8,128)S(1)} %get-tuple-element.275, s32[]{:T(128)} %get-tuple-element.268), kind=kOutput, calls=%fused_computation.25.clone.1.clone | convolution fusion | flops 404942848 | bytes 81924 | tf_op jit(solution)/shard_map/while/body/eval_jaxpr/dot_general | solution.py:47
  364.8 4.4 %fusion.73 = f32[4096]{0:T(1024)S(1)} fusion(s32[4096]{0:T(1024)S(1)} %add_select_fusion.7, s32[4096]{0:T(1024)S(1)} %bitcast.57, f32[16,16,512]{2,1,0:T(8,128)S(1)} %get-tuple-element.275, s32[]{:T(128)} %get-tuple-element.268), kind=kOutput, calls=%fused_computation.25.clone.1.clone | convolution fusion | flops 404942848 | bytes 81924 | tf_op jit(solution)/shard_map/while/body/eval_jaxpr/dot_general | solution.py:47
  370.7 4.4 %fusion.73 = f32[4096]{0:T(1024)S(1)} fusion(s32[4096]{0:T(1024)S(1)} %add_select_fusion.7, s32[4096]{0:T(1024)S(1)} %bitcast.57, f32[16,16,512]{2,1,0:T(8,128)S(1)} %get-tuple-element.275, s32[]{:T(128)} %get-tuple-element.268), kind=kOutput, calls=%fused_computation.25.clone.1.clone | convolution fusion | flops 404942848 | bytes 81924 | tf_op jit(solution)/shard_map/while/body/eval_jaxpr/dot_general | solution.py:47
  (189 shorter events, 190.3 us)
Async XLA Ops:
  7.2 128.5 %reduce-scatter.2.cloned.1.call-start = ((), (), s32[]{:S(2)}) async-start(), calls=%async_computation.1 | async-start | bytes 557056 | tf_op jit(solution)/shard_map/reduce_scatter | solution.py:91
  136.4 10.4 %collective-permute-start = (f32[1,512]{1,0:T(1,128)S(1)}, f32[1,512]{1,0:T(1,128)S(1)}, u32[]{:S(2)}, u32[]{:S(2)}) collective-permute-start(f32[1,512]{1,0:T(1,128)S(1)} %get-tuple-element.164), channel_id=1, source_target_pairs={{4,0},{8,4},{12,8},{16,12},{20,16},{24,20},{28,24},{32,28},{36,32}... | collective-permute-start | bytes 6152 | tf_op jit(solution)/shard_map/ppermute | solution.py:17
  144.2 6.1 %collective-permute-start.1 = (f32[1,512]{1,0:T(1,128)S(1)}, f32[1,512]{1,0:T(1,128)S(1)}, u32[]{:S(2)}, u32[]{:S(2)}) collective-permute-start(f32[1,512]{1,0:T(1,128)S(1)} %get-tuple-element.163), channel_id=1, source_target_pairs={{0,4},{4,8},{8,12},{12,16},{16,20},{20,24},{24,28},{28,32},{32,36}... | collective-permute-start | bytes 6152 | tf_op jit(solution)/shard_map/ppermute | solution.py:14
  151.1 5.3 %collective-permute-start.2 = (f32[18,1]{1,0:T(8,128)S(1)}, f32[18,1]{1,0:T(8,128)S(1)}, u32[]{:S(2)}, u32[]{:S(2)}) collective-permute-start(f32[18,1]{1,0:T(8,128)S(1)} %get-tuple-element.151), channel_id=1, source_target_pairs={{1,0},{2,1},{3,2},{5,4},{6,5},{7,6},{9,8},{10,9},{11,10},{13,12},{... | collective-permute-start | bytes 224 | tf_op jit(solution)/shard_map/ppermute | solution.py:17
  153.3 4.4 %collective-permute-start.3 = (f32[18,1]{1,0:T(8,128)S(1)}, f32[18,1]{1,0:T(8,128)S(1)}, u32[]{:S(2)}, u32[]{:S(2)}) collective-permute-start(f32[18,1]{1,0:T(8,128)S(1)} %get-tuple-element.152), channel_id=1, source_target_pairs={{0,1},{1,2},{2,3},{4,5},{5,6},{6,7},{8,9},{9,10},{10,11},{12,13},{... | collective-permute-start | bytes 224 | tf_op jit(solution)/shard_map/ppermute | solution.py:14
  161.3 5.5 %collective-permute-start.4 = (f32[1,512]{1,0:T(1,128)S(1)}, f32[1,512]{1,0:T(1,128)S(1)}, u32[]{:S(2)}, u32[]{:S(2)}) collective-permute-start(f32[1,512]{1,0:T(1,128)S(1)} %get-tuple-element.162), channel_id=1, source_target_pairs={{4,0},{8,4},{12,8},{16,12},{20,16},{24,20},{28,24},{32,28},{36,32}... | collective-permute-start | bytes 6152 | tf_op jit(solution)/shard_map/ppermute | solution.py:17
  164.9 6.1 %collective-permute-start.5 = (f32[1,512]{1,0:T(1,128)S(1)}, f32[1,512]{1,0:T(1,128)S(1)}, u32[]{:S(2)}, u32[]{:S(2)}) collective-permute-start(f32[1,512]{1,0:T(1,128)S(1)} %get-tuple-element.161), channel_id=1, source_target_pairs={{0,4},{4,8},{8,12},{12,16},{16,20},{20,24},{24,28},{28,32},{32,36}... | collective-permute-start | bytes 6152 | tf_op jit(solution)/shard_map/ppermute | solution.py:14
  171.1 5.3 %collective-permute-start.6 = (f32[18,1]{1,0:T(8,128)S(1)}, f32[18,1]{1,0:T(8,128)S(1)}, u32[]{:S(2)}, u32[]{:S(2)}) collective-permute-start(f32[18,1]{1,0:T(8,128)S(1)} %get-tuple-element.149), channel_id=1, source_target_pairs={{1,0},{2,1},{3,2},{5,4},{6,5},{7,6},{9,8},{10,9},{11,10},{13,12},{... | collective-permute-start | bytes 224 | tf_op jit(solution)/shard_map/ppermute | solution.py:17
  173.3 4.4 %collective-permute-start.7 = (f32[18,1]{1,0:T(8,128)S(1)}, f32[18,1]{1,0:T(8,128)S(1)}, u32[]{:S(2)}, u32[]{:S(2)}) collective-permute-start(f32[18,1]{1,0:T(8,128)S(1)} %get-tuple-element.150), channel_id=1, source_target_pairs={{0,1},{1,2},{2,3},{4,5},{5,6},{6,7},{8,9},{9,10},{10,11},{12,13},{... | collective-permute-start | bytes 224 | tf_op jit(solution)/shard_map/ppermute | solution.py:14
  180.3 5.3 %collective-permute-start.8 = (f32[1,512]{1,0:T(1,128)S(1)}, f32[1,512]{1,0:T(1,128)S(1)}, u32[]{:S(2)}, u32[]{:S(2)}) collective-permute-start(f32[1,512]{1,0:T(1,128)S(1)} %get-tuple-element.160), channel_id=1, source_target_pairs={{4,0},{8,4},{12,8},{16,12},{20,16},{24,20},{28,24},{32,28},{36,32}... | collective-permute-start | bytes 6152 | tf_op jit(solution)/shard_map/ppermute | solution.py:17
  183.7 6.1 %collective-permute-start.9 = (f32[1,512]{1,0:T(1,128)S(1)}, f32[1,512]{1,0:T(1,128)S(1)}, u32[]{:S(2)}, u32[]{:S(2)}) collective-permute-start(f32[1,512]{1,0:T(1,128)S(1)} %get-tuple-element.159), channel_id=1, source_target_pairs={{0,4},{4,8},{8,12},{12,16},{16,20},{20,24},{24,28},{28,32},{32,36}... | collective-permute-start | bytes 6152 | tf_op jit(solution)/shard_map/ppermute | solution.py:14
  189.9 5.3 %collective-permute-start.10 = (f32[18,1]{1,0:T(8,128)S(1)}, f32[18,1]{1,0:T(8,128)S(1)}, u32[]{:S(2)}, u32[]{:S(2)}) collective-permute-start(f32[18,1]{1,0:T(8,128)S(1)} %get-tuple-element.147), channel_id=1, source_target_pairs={{1,0},{2,1},{3,2},{5,4},{6,5},{7,6},{9,8},{10,9},{11,10},{13,12},{... | collective-permute-start | bytes 224 | tf_op jit(solution)/shard_map/ppermute | solution.py:17
  191.8 4.4 %collective-permute-start.11 = (f32[18,1]{1,0:T(8,128)S(1)}, f32[18,1]{1,0:T(8,128)S(1)}, u32[]{:S(2)}, u32[]{:S(2)}) collective-permute-start(f32[18,1]{1,0:T(8,128)S(1)} %get-tuple-element.148), channel_id=1, source_target_pairs={{0,1},{1,2},{2,3},{4,5},{5,6},{6,7},{8,9},{9,10},{10,11},{12,13},{... | collective-permute-start | bytes 224 | tf_op jit(solution)/shard_map/ppermute | solution.py:14
  199.4 5.3 %collective-permute-start.12 = (f32[1,512]{1,0:T(1,128)S(1)}, f32[1,512]{1,0:T(1,128)S(1)}, u32[]{:S(2)}, u32[]{:S(2)}) collective-permute-start(f32[1,512]{1,0:T(1,128)S(1)} %get-tuple-element.158), channel_id=1, source_target_pairs={{4,0},{8,4},{12,8},{16,12},{20,16},{24,20},{28,24},{32,28},{36,32}... | collective-permute-start | bytes 6152 | tf_op jit(solution)/shard_map/ppermute | solution.py:17
  202.5 6.1 %collective-permute-start.13 = (f32[1,512]{1,0:T(1,128)S(1)}, f32[1,512]{1,0:T(1,128)S(1)}, u32[]{:S(2)}, u32[]{:S(2)}) collective-permute-start(f32[1,512]{1,0:T(1,128)S(1)} %get-tuple-element.157), channel_id=1, source_target_pairs={{0,4},{4,8},{8,12},{12,16},{16,20},{20,24},{24,28},{28,32},{32,36}... | collective-permute-start | bytes 6152 | tf_op jit(solution)/shard_map/ppermute | solution.py:14
  208.7 5.3 %collective-permute-start.14 = (f32[18,1]{1,0:T(8,128)S(1)}, f32[18,1]{1,0:T(8,128)S(1)}, u32[]{:S(2)}, u32[]{:S(2)}) collective-permute-start(f32[18,1]{1,0:T(8,128)S(1)} %get-tuple-element.145), channel_id=1, source_target_pairs={{1,0},{2,1},{3,2},{5,4},{6,5},{7,6},{9,8},{10,9},{11,10},{13,12},{... | collective-permute-start | bytes 224 | tf_op jit(solution)/shard_map/ppermute | solution.py:17
  210.7 4.4 %collective-permute-start.15 = (f32[18,1]{1,0:T(8,128)S(1)}, f32[18,1]{1,0:T(8,128)S(1)}, u32[]{:S(2)}, u32[]{:S(2)}) collective-permute-start(f32[18,1]{1,0:T(8,128)S(1)} %get-tuple-element.146), channel_id=1, source_target_pairs={{0,1},{1,2},{2,3},{4,5},{5,6},{6,7},{8,9},{9,10},{10,11},{12,13},{... | collective-permute-start | bytes 224 | tf_op jit(solution)/shard_map/ppermute | solution.py:14
  217.7 5.3 %collective-permute-start.16 = (f32[1,512]{1,0:T(1,128)S(1)}, f32[1,512]{1,0:T(1,128)S(1)}, u32[]{:S(2)}, u32[]{:S(2)}) collective-permute-start(f32[1,512]{1,0:T(1,128)S(1)} %get-tuple-element.156), channel_id=1, source_target_pairs={{4,0},{8,4},{12,8},{16,12},{20,16},{24,20},{28,24},{32,28},{36,32}... | collective-permute-start | bytes 6152 | tf_op jit(solution)/shard_map/ppermute | solution.py:17
  220.8 6.1 %collective-permute-start.17 = (f32[1,512]{1,0:T(1,128)S(1)}, f32[1,512]{1,0:T(1,128)S(1)}, u32[]{:S(2)}, u32[]{:S(2)}) collective-permute-start(f32[1,512]{1,0:T(1,128)S(1)} %get-tuple-element.155), channel_id=1, source_target_pairs={{0,4},{4,8},{8,12},{12,16},{16,20},{20,24},{24,28},{28,32},{32,36}... | collective-permute-start | bytes 6152 | tf_op jit(solution)/shard_map/ppermute | solution.py:14
  227.0 5.3 %collective-permute-start.18 = (f32[18,1]{1,0:T(8,128)S(1)}, f32[18,1]{1,0:T(8,128)S(1)}, u32[]{:S(2)}, u32[]{:S(2)}) collective-permute-start(f32[18,1]{1,0:T(8,128)S(1)} %get-tuple-element.143), channel_id=1, source_target_pairs={{1,0},{2,1},{3,2},{5,4},{6,5},{7,6},{9,8},{10,9},{11,10},{13,12},{... | collective-permute-start | bytes 224 | tf_op jit(solution)/shard_map/ppermute | solution.py:17
  236.0 5.3 %collective-permute-start.20 = (f32[1,512]{1,0:T(1,128)S(1)}, f32[1,512]{1,0:T(1,128)S(1)}, u32[]{:S(2)}, u32[]{:S(2)}) collective-permute-start(f32[1,512]{1,0:T(1,128)S(1)} %get-tuple-element.154), channel_id=1, source_target_pairs={{4,0},{8,4},{12,8},{16,12},{20,16},{24,20},{28,24},{32,28},{36,32}... | collective-permute-start | bytes 6152 | tf_op jit(solution)/shard_map/ppermute | solution.py:17
  239.1 6.1 %collective-permute-start.21 = (f32[1,512]{1,0:T(1,128)S(1)}, f32[1,512]{1,0:T(1,128)S(1)}, u32[]{:S(2)}, u32[]{:S(2)}) collective-permute-start(f32[1,512]{1,0:T(1,128)S(1)} %get-tuple-element.153), channel_id=1, source_target_pairs={{0,4},{4,8},{8,12},{12,16},{16,20},{20,24},{24,28},{28,32},{32,36}... | collective-permute-start | bytes 6152 | tf_op jit(solution)/shard_map/ppermute | solution.py:14
  245.3 5.3 %collective-permute-start.22 = (f32[18,1]{1,0:T(8,128)S(1)}, f32[18,1]{1,0:T(8,128)S(1)}, u32[]{:S(2)}, u32[]{:S(2)}) collective-permute-start(f32[18,1]{1,0:T(8,128)S(1)} %get-tuple-element.141), channel_id=1, source_target_pairs={{1,0},{2,1},{3,2},{5,4},{6,5},{7,6},{9,8},{10,9},{11,10},{13,12},{... | collective-permute-start | bytes 224 | tf_op jit(solution)/shard_map/ppermute | solution.py:17
  247.2 4.4 %collective-permute-start.23 = (f32[18,1]{1,0:T(8,128)S(1)}, f32[18,1]{1,0:T(8,128)S(1)}, u32[]{:S(2)}, u32[]{:S(2)}) collective-permute-start(f32[18,1]{1,0:T(8,128)S(1)} %get-tuple-element.142), channel_id=1, source_target_pairs={{0,1},{1,2},{2,3},{4,5},{5,6},{6,7},{8,9},{9,10},{10,11},{12,13},{... | collective-permute-start | bytes 224 | tf_op jit(solution)/shard_map/ppermute | solution.py:14
  (5 other events, 362.0 us)
Sparse Core Ops, SparseCore 0:
  79.1 56.5 reduce-scatter.1
where the time goes:
time: 386 us; the launch traced here: 383 us
  matrix products  125 us (32%)
  waiting for transfers between devices  87.3 us (23%)
  starting transfers between devices  68 us (18%)
  other arithmetic  49.7 us (13%)
  blocking collectives  29.6 us (8%)
  between operations  14.4 us (4%)
  local copies, waits for them, and re-layouts  8.07 us (2%)
    dot_general x16, matrix products, pick_strip(): lax.dot_general(field, col_table, (((1,), (1,)), ((), ())), precision=lax...  71.1 us
    reduce_scatter x1, waiting for transfers between devices, local(): lax.psum_scatter(partial_value, 'shots', scatter_dimension=0, tiled=True)[0]  56.7 us
    dot_general x16, matrix products, deposit_strip(): jnp.dot(row_table * dose[None, :], col_table, precision=lax.Precision.HIG...  54 us
    ppermute x12, starting transfers between devices, extended(): lax.ppermute(lax.slice_in_dim(block, 0, width, axis=dim), axis, backward)  36 us
    ppermute x12, starting transfers between devices, extended(): lax.ppermute(lax.slice_in_dim(block, block.shape[dim] - width, None, axis...  31.9 us
    select_n x32, other arithmetic, one_hots(): row_ids = cells // cols  31.8 us
    ppermute x12, waiting for transfers between devices, extended(): lax.ppermute(lax.slice_in_dim(block, block.shape[dim] - width, None, axis...  30.5 us
    all_gather x1, blocking collectives, local(): whole = lax.all_gather(adjoint, 'shots', axis=0, tiled=True)  29.6 us
  transfers between devices with their start and end apart: 25, of which 13 were waited for; matrix products, arithmetic and copies ran while one was open for 0% of the time, Pallas kernels for 0%

commit v1 on v0

v1 whole, which is shorter than its diff:
```python
import functools

import jax
import jax.numpy as jnp
from jax import lax
from jax.experimental import pallas as pl
from jax.experimental.pallas import tpu as pltpu
from jax.sharding import PartitionSpec as P

STEPS = 3
SPAN = 512
LANES = 128
VMEM = pl.BlockSpec(memory_space=pltpu.VMEM)
SMEM = pl.BlockSpec(memory_space=pltpu.SMEM)
PARAMS = pltpu.CompilerParams(vmem_limit_bytes=32 << 20)
F32 = jnp.float32
BF16 = jnp.bfloat16


def f32(*shape):
    return jax.ShapeDtypeStruct(shape, F32)


def rows_of(value, kind):
    return jnp.broadcast_to(value, (16, value.shape[1])).astype(kind)


def hot(index, groups, filled):
    width = index.shape[1]
    ids = rows_of(index, jnp.int16)
    iota = lax.broadcasted_iota(jnp.int16, (16, width), 0)
    masks = [ids == iota + jnp.int16(16 * g) for g in range(groups)]
    zero = jnp.bfloat16(0)
    return [jnp.concatenate([jnp.where(m, f, zero) for m in masks], axis=0) for f in filled]


def split(cell):
    return ((cell >> 7) & 3) * 16 + (cell >> 9), cell & 127


def deposit_kernel(side_ref, counts_ref, cells_ref, dose_ref, out_ref):
    side = side_ref[0]
    slots = cells_ref.shape[1]

    def strip(j, carry):
        o = 2 * j + side
        count = counts_ref[o]
        total = jnp.zeros((2 * 64, LANES), F32)
        for k in range(0, slots, SPAN):
            cell = cells_ref[pl.ds(o, 1), k : k + SPAN]
            slot = lax.broadcasted_iota(jnp.int32, (1, SPAN), 1) + k
            dose = jnp.where(slot < count, dose_ref[pl.ds(o, 1), k : k + SPAN], 0.0)
            high = dose.astype(BF16).astype(F32)
            chunk, lane = split(cell)
            rows = hot(chunk, 4, [rows_of(high, BF16), rows_of(dose - high, BF16)])
            (cols,) = hot(lane, 8, [jnp.bfloat16(1)])
            total = total + lax.dot_general(
                jnp.concatenate(rows, axis=0),
                cols,
                (((1,), (1,)), ((), ())),
                preferred_element_type=F32,
            )
        both = total[:64] + total[64:]
        for q in range(4):
            out_ref[j, :, q * LANES : (q + 1) * LANES] = both[16 * q : 16 * q + 16]
        return carry

    lax.fori_loop(0, out_ref.shape[0], strip, 0)


def deposit(side, counts, cells, dose):
    return pl.pallas_call(
        deposit_kernel,
        out_shape=f32(8, 16, 512),
        in_specs=[SMEM, SMEM, VMEM, VMEM],
        out_specs=VMEM,
        compiler_params=PARAMS,
        cost_estimate=pl.CostEstimate(flops=1 << 30, bytes_accessed=1 << 19, transcendentals=0),
        name="deposit",
    )(side, counts, cells, dose)


def gather_kernel(coef_ref, parts_ref, materials_ref, target_ref, mid_ref, left_ref, right_ref):
    strip = parts_ref[0]
    for z in range(1, parts_ref.shape[0]):
        strip = strip + parts_ref[z]
    materials = materials_ref[...]
    spread = jnp.zeros(materials.shape, F32)
    for index in range(coef_ref.shape[0]):
        spread = jnp.where(materials == index, coef_ref[index], spread)
    for i, value in enumerate((strip, spread, target_ref[...])):
        mid_ref[i] = value
        left_ref[i] = value[:, :LANES]
        right_ref[i] = value[:, -LANES:]


def widen_kernel(mid_ref, left_ref, right_ref, wide_ref, top_ref, bottom_ref):
    for i in range(3):
        wide = jnp.concatenate([left_ref[i], mid_ref[i], right_ref[i]], axis=1)
        wide_ref[i] = wide
        if i == 0:
            top_ref[:8] = wide[:8]
            bottom_ref[:8] = wide[8:]
        elif i == 1:
            top_ref[8:13] = wide[:5]
            bottom_ref[11:] = wide[11:]
        else:
            top_ref[13:] = wide[:3]
            bottom_ref[8:11] = wide[13:]


def neighbours(field):
    height, width = field.shape
    return (
        pltpu.roll(field, 1, 0)
        + pltpu.roll(field, height - 1, 0)
        + pltpu.roll(field, 1, 1)
        + pltpu.roll(field, width - 1, 1)
    )


def blur_kernel(wide_ref, above_ref, below_ref, exposure_ref, adjoint_ref):
    width = wide_ref.shape[2]
    blank = lambda rows: jnp.zeros((rows, width), F32)
    field = jnp.concatenate([above_ref[:8], wide_ref[0], below_ref[:8]], axis=0)
    spread = jnp.concatenate(
        [blank(3), above_ref[11:], wide_ref[1], below_ref[8:13], blank(3)], axis=0
    )
    target = jnp.concatenate(
        [blank(5), above_ref[8:11], wide_ref[2], below_ref[13:], blank(5)], axis=0
    )
    for step in range(STEPS):
        field = field + spread * (neighbours(field) - 4.0 * field)
    exposure_ref[...] = field[8:24, LANES:-LANES]
    field = field - target
    for step in range(STEPS):
        weighted = spread * field
        field = field + neighbours(weighted) - 4.0 * weighted
    for q in range(4):
        adjoint_ref[16 * q : 16 * q + 16] = field[8:24, (q + 1) * LANES : (q + 2) * LANES]


def pick_kernel(counts_ref, cells_ref, table_ref, out_ref):
    slots = cells_ref.shape[1]

    def strip(o, carry):
        table = table_ref[pl.ds(pl.multiple_of(o * 64, 64), 64), :]
        high = table.astype(BF16)
        low = (table - high.astype(F32)).astype(BF16)
        both = jnp.concatenate([high, low], axis=0)
        count = counts_ref[o]
        for k in range(0, slots, SPAN):
            chunk, lane = split(cells_ref[pl.ds(o, 1), k : k + SPAN])
            (cols,) = hot(lane, 8, [jnp.bfloat16(1)])
            across = jnp.dot(both, cols, preferred_element_type=F32)
            across = across[:64] + across[64:]
            iota = lax.broadcasted_iota(jnp.int32, (8, SPAN), 0)
            chosen = jnp.broadcast_to(chunk, (8, SPAN))
            value = jnp.zeros((8, SPAN), F32)
            for g in range(8):
                value = jnp.where(chosen == iota + 8 * g, across[8 * g : 8 * g + 8], value)
            value = jnp.sum(value, axis=0, keepdims=True)
            slot = lax.broadcasted_iota(jnp.int32, (1, SPAN), 1) + k
            out_ref[pl.ds(o, 1), k : k + SPAN] = jnp.where(slot < count, value, 0.0)
        return carry

    lax.fori_loop(0, cells_ref.shape[0], strip, 0)


def pick(counts, cells, table):
    return pl.pallas_call(
        pick_kernel,
        out_shape=f32(*cells.shape),
        in_specs=[SMEM, VMEM, VMEM],
        out_specs=VMEM,
        compiler_params=PARAMS,
        name="pick",
    )(counts, cells, table)


def shifted(value, axes, count, by):
    return lax.ppermute(
        value, axes, [(i, i + by) for i in range(count) if 0 <= i + by < count]
    )


def local(shot_cells, shot_dose, shot_counts, materials, coefficients, target):
    cells, dose, counts = shot_cells[0, 0, 0], shot_dose[0, 0, 0], shot_counts[0, 0, 0]
    shots = lax.axis_size("shots")
    core = lax.axis_index("shots") % 2
    side = jnp.reshape(core, (1,)).astype(jnp.int32)
    away = deposit(1 - side, counts, cells, dose)
    arrived = lax.ppermute(away, "shots", [(i, i ^ 1) for i in range(shots)])
    own = deposit(side, counts, cells, dose)
    paired = own + arrived
    groups = [[2 * z + c for z in range(shots // 2)] for c in range(2)]
    parts = lax.all_to_all(paired, "shots", 0, 0, axis_index_groups=groups, tiled=True)
    mid, left, right = pl.pallas_call(
        gather_kernel,
        out_shape=(f32(3, 16, 512), f32(3, 16, LANES), f32(3, 16, LANES)),
        in_specs=[SMEM, VMEM, VMEM, VMEM],
        out_specs=(VMEM,) * 3,
        compiler_params=PARAMS,
        name="gather",
    )(coefficients, parts, materials, target)
    columns = lax.axis_size("gx")
    from_left = shifted(right, "gx", columns, 1)
    from_right = shifted(left, "gx", columns, -1)
    wide, top, bottom = pl.pallas_call(
        widen_kernel,
        out_shape=(f32(3, 16, 768), f32(16, 768), f32(16, 768)),
        in_specs=[VMEM] * 3,
        out_specs=(VMEM,) * 3,
        compiler_params=PARAMS,
        name="widen",
    )(mid, from_left, from_right)
    strips = shots * lax.axis_size("gy")
    above = shifted(bottom, ("shots", "gy"), strips, 1)
    below = shifted(top, ("shots", "gy"), strips, -1)
    exposure, adjoint = pl.pallas_call(
        blur_kernel,
        out_shape=(f32(16, 512), f32(64, LANES)),
        in_specs=[VMEM] * 3,
        out_specs=(VMEM,) * 2,
        compiler_params=PARAMS,
        name="blur",
    )(wide, above, below)
    table = lax.all_gather(adjoint, "shots", axis=0, tiled=True)
    shot_grad = pick(counts, cells, table)
    return (exposure, shot_grad[None, None, None])


def solution(mesh):
    placed = (
        P("shots", "gy", "gx", None, None),
        P("shots", "gy", "gx", None, None),
        P("shots", "gy", "gx", None),
        P(("shots", "gy"), "gx"),
        P(),
        P(("shots", "gy"), "gx"),
    )
    return jax.shard_map(
        local,
        mesh=mesh,
        in_specs=placed,
        out_specs=(P(("shots", "gy"), "gx"), P("shots", "gy", "gx", None, None)),
        check_vma=False,
    )
```

time: 386 us -> 79 us (0.20)
  matrix products: 125 us -> 0 us
  waiting for transfers between devices: 87.3 us -> 3.3 us
  starting transfers between devices: 68 us -> 14.4 us
  other arithmetic: 49.7 us -> 0.04 us
  Pallas kernels: 0 us -> 18.2 us
  between operations: 14.4 us -> 0.77 us
  blocking collectives: 29.6 us -> 38.2 us
  local copies, waits for them, and re-layouts: 8.07 us -> 2.57 us
    dot_general x32 -> x0, matrix products: 125 us -> none  [the longest x16 71.1 us: pick_strip(): lax.dot_general(field, col_table, (((1,), (1,)), ((), ())), precision=lax...]
    reduce_scatter x1 -> x0, waiting for transfers between devices: 56.7 us -> none  [local(): lax.psum_scatter(partial_value, 'shots', scatter_dimension=0, tiled=True)[0]]
    ppermute x24 -> x5, starting transfers between devices: 67.9 us -> 14.4 us  [the longest x4 13.6 us: shifted(): lax.ppermute(value, axes, [(i, i + by) for i in range(count) if 0 <= i +...]
    select_n x65 -> x0, other arithmetic: 33.2 us -> none  [the longest x32 31.8 us: one_hots(): row_ids = cells // cols]
    ppermute x24 -> x5, waiting for transfers between devices: 30.5 us -> 3.3 us  [the longest x4 3.3 us: shifted(): lax.ppermute(value, axes, [(i, i + by) for i in range(count) if 0 <= i +...]
    all_to_all x0 -> x1, blocking collectives: none -> 20.3 us  [local(): lax.all_to_all(paired, 'shots', 0, 0, axis_index_groups=groups, tiled=True)]
    pallas_call x0 -> x6, Pallas kernels: none -> 18.2 us  [the longest x2 8.28 us: deposit(): pl.pallas_call(deposit_kernel, out_shape=f32(8, 16, 512), in_specs=[SMEM,...]
    all_gather x1, blocking collectives: 29.6 us -> 17.9 us  [local(): table = lax.all_gather(adjoint, 'shots', axis=0, tiled=True)]
  transfers between devices with their start and end apart: 25 -> 5, of which waited for: 13 -> 2; matrix products, arithmetic and copies ran while one was open for 0% -> 0% of each run, Pallas kernels for 0% -> 5%
where the time goes in v1:
time: 79 us; the launch traced here: 77.5 us
  blocking collectives  38.2 us (48%)
  Pallas kernels  18.2 us (23%)
  starting transfers between devices  14.4 us (18%)
  waiting for transfers between devices  3.3 us (4%)
  local copies, waits for them, and re-layouts  2.57 us (3%)
    all_to_all x1, blocking collectives, local(): lax.all_to_all(paired, 'shots', 0, 0, axis_index_groups=groups, tiled=True)  20.3 us
    all_gather x1, blocking collectives, local(): table = lax.all_gather(adjoint, 'shots', axis=0, tiled=True)  17.9 us
    ppermute x4, starting transfers between devices, shifted(): lax.ppermute(value, axes, [(i, i + by) for i in range(count) if 0 <= i +...  13.6 us
    pallas_call x2, Pallas kernels, deposit(): pl.pallas_call(deposit_kernel, out_shape=f32(8, 16, 512), in_specs=[SMEM,...  8.28 us
    pallas_call x1, Pallas kernels, pick(): pl.pallas_call(pick_kernel, out_shape=f32(*cells.shape), in_specs=[SMEM,...  8.25 us
    ppermute x4, waiting for transfers between devices, shifted(): lax.ppermute(value, axes, [(i, i + by) for i in range(count) if 0 <= i +...  3.3 us
    unnamed x14, local copies, waits for them, and re-layouts  2.57 us
  transfers between devices with their start and end apart: 5, of which 2 were waited for; matrix products, arithmetic and copies ran while one was open for 0% of the time, Pallas kernels for 5%

profile of v1, /device:TPU:5, one launch (start us, length us, event | category | flops | bytes accessed | tf_op | source)
XLA Modules:
  0.0 77.5 jit_solution(2676674373545606759)
XLA Ops:
  0.7 0.6 copy-done.5
  1.3 0.9 %copy-done = s32[1,1,1,16,4096]{4,3,2,1,0:T(8,128)S(1)} copy-done((s32[1,1,1,16,4096]{4,3,2,1,0:T(8,128)S(1)}, s32[1,1,1,16,4096]{4,3,2,1,0:T(8,128)}, u32[]{:S(2)}) %copy-start) | copy-done | bytes 262168
  2.3 0.9 %copy-done.6 = f32[1,1,1,16,4096]{4,3,2,1,0:T(8,128)S(1)} copy-done((f32[1,1,1,16,4096]{4,3,2,1,0:T(8,128)S(1)}, f32[1,1,1,16,4096]{4,3,2,1,0:T(8,128)}, u32[]{:S(2)}) %copy-start.6) | copy-done | bytes 262168
  3.2 4.1 %deposit.3 = f32[8,16,512]{2,1,0:T(8,128)S(1)} custom-call(s32[1]{0:T(128)S(6)} %sub.3.side_ref, s32[16]{0:T(128)S(1)} %bitcast.8, s32[16,4096]{1,0:T(8,128)S(1)} %bitcast.5, f32[16,4096]{1,0:T(8,128)S(1)} %bitcast.11), custom_call_target="tpu_custom_call" | custom-call | flops 1073741824 | bytes 524288 | tf_op jit(solution)/shard_map/deposit/pallas_call | solution.py:72
  7.3 0.8 %collective-permute-start = (f32[8,16,512]{2,1,0:T(8,128)S(1)}, f32[8,16,512]{2,1,0:T(8,128)S(1)}, u32[]{:S(2)}, u32[]{:S(2)}) collective-permute-start(f32[8,16,512]{2,1,0:T(8,128)S(1)} %deposit.3), channel_id=1, source_target_pairs={{0,16},{16,0},{32,48},{48,32},{64,80},{80,64},{96,112},{112,96},{1... | collective-permute-start | bytes 786440 | tf_op jit(solution)/shard_map/ppermute | solution.py:193
  8.1 4.2 %deposit.2 = f32[8,16,512]{2,1,0:T(8,128)S(1)} custom-call(s32[1]{0:T(128)} %bitcast.side_ref, s32[16]{0:T(128)S(1)} %bitcast.9, s32[16,4096]{1,0:T(8,128)S(1)} %bitcast.6, f32[16,4096]{1,0:T(8,128)S(1)} %bitcast.12), custom_call_target="tpu_custom_call" | custom-call | flops 1073741824 | bytes 524288 | tf_op jit(solution)/shard_map/deposit/pallas_call | solution.py:72
  12.3 0.0 collective-permute-done
  12.4 0.0 copy-start.2
  12.4 0.0 copy-start.3
  12.4 0.0 copy-start.4
  12.4 20.3 %all_to_all.5.parts_ref = f32[8,16,512]{2,1,0:T(8,128)S(1)} all-to-all(f32[8,16,512]{2,1,0:T(8,128)S(1)} %add.8), channel_id=1, replica_groups={{0,32,64,96,128,160,192,224},{16,48,80,112,144,176,208,240},{1,33,65,97..., dimensions={0} | all-to-all | bytes 524288 | tf_op jit(solution)/shard_map/all_to_all | solution.py:197
  32.7 0.0 copy-done.3
  32.7 0.6 gather.1
  33.3 2.9 %collective-permute-start.1 = (f32[3,16,128]{2,1,0:T(8,128)S(1)}, f32[3,16,128]{2,1,0:T(8,128)S(1)}, u32[]{:S(2)}, u32[]{:S(2)}) collective-permute-start(f32[3,16,128]{2,1,0:T(8,128)S(1)} %get-tuple-element.11), channel_id=1, source_target_pairs={{0,1},{1,2},{2,3},{4,5},{5,6},{6,7},{8,9},{9,10},{10,11},{12,13},{... | collective-permute-start | bytes 73736 | tf_op jit(solution)/shard_map/ppermute | solution.py:182
  36.2 2.4 %collective-permute-start.2 = (f32[3,16,128]{2,1,0:T(8,128)S(1)}, f32[3,16,128]{2,1,0:T(8,128)S(1)}, u32[]{:S(2)}, u32[]{:S(2)}) collective-permute-start(f32[3,16,128]{2,1,0:T(8,128)S(1)} %get-tuple-element.12), channel_id=1, source_target_pairs={{1,0},{2,1},{3,2},{5,4},{6,5},{7,6},{9,8},{10,9},{11,10},{13,12},{... | collective-permute-start | bytes 73736 | tf_op jit(solution)/shard_map/ppermute | solution.py:182
  38.6 0.0 collective-permute-done.1.left_ref
  38.6 2.2 %collective-permute-done.2.right_ref = f32[3,16,128]{2,1,0:T(8,128)S(1)} collective-permute-done((f32[3,16,128]{2,1,0:T(8,128)S(1)}, f32[3,16,128]{2,1,0:T(8,128)S(1)}, u32[]{:S(2)}, u32[]{:S(2)}) %collective-permute-start.2) | collective-permute-done | bytes 24608 | tf_op jit(solution)/shard_map/ppermute | solution.py:182
  40.8 3.2 %collective-permute-start.3 = (f32[16,768]{1,0:T(8,128)S(1)}, f32[16,768]{1,0:T(8,128)S(1)}, u32[]{:S(2)}, u32[]{:S(2)}) collective-permute-start(f32[16,768]{1,0:T(8,128)S(1)} %get-tuple-element.14), channel_id=1, source_target_pairs={{0,4},{4,8},{8,12},{12,16},{16,20},{20,24},{24,28},{28,32},{32,36}... | collective-permute-start | bytes 147464 | tf_op jit(solution)/shard_map/ppermute | solution.py:182
  44.0 5.1 %collective-permute-start.4 = (f32[16,768]{1,0:T(8,128)S(1)}, f32[16,768]{1,0:T(8,128)S(1)}, u32[]{:S(2)}, u32[]{:S(2)}) collective-permute-start(f32[16,768]{1,0:T(8,128)S(1)} %get-tuple-element.15), channel_id=1, source_target_pairs={{4,0},{8,4},{12,8},{16,12},{20,16},{24,20},{28,24},{32,28},{36,32}... | collective-permute-start | bytes 147464 | tf_op jit(solution)/shard_map/ppermute | solution.py:182
  49.1 0.0 collective-permute-done.3.above_ref
  49.1 1.1 %collective-permute-done.4.below_ref = f32[16,768]{1,0:T(8,128)S(1)} collective-permute-done((f32[16,768]{1,0:T(8,128)S(1)}, f32[16,768]{1,0:T(8,128)S(1)}, u32[]{:S(2)}, u32[]{:S(2)}) %collective-permute-start.4) | collective-permute-done | bytes 49184 | tf_op jit(solution)/shard_map/ppermute | solution.py:182
  50.3 1.1 %blur.1 = (f32[16,512]{1,0:T(8,128)}, f32[64,128]{1,0:T(8,128)S(1)}) custom-call(f32[3,16,768]{2,1,0:T(8,128)S(1)} %get-tuple-element.13.wide_ref, f32[16,768]{1,0:T(8,128)S(1)} %collective-permute-done.3.above_ref, f32[16,768]{1,0:T(8,128)S(1)} %collective-permute-done.4.below_ref), custom_call_target="tpu_custom_call" | custom-call | tf_op jit(solution)/shard_map/blur/pallas_call | solution.py:220
  51.4 17.9 %all_gather.3.table_ref = f32[1024,128]{1,0:T(8,128)S(1)} all-gather(f32[64,128]{1,0:T(8,128)S(1)} %get-tuple-element.17), channel_id=1, replica_groups=mesh['shots'=16,'gy'=4,'gx'=4] {'shots'}, dimensions={0}, use_global_device_ids=true | all-gather | bytes 557056 | tf_op jit(solution)/shard_map/all_gather | solution.py:228
  69.3 8.3 %pick.1 = f32[16,4096]{1,0:T(8,128)} custom-call(s32[16]{0:T(128)S(1)} %bitcast.10, s32[16,4096]{1,0:T(8,128)S(1)} %bitcast.7, f32[1024,128]{1,0:T(8,128)S(1)} %all_gather.3.table_ref), custom_call_target="tpu_custom_call" | custom-call | tf_op jit(solution)/shard_map/pick/pallas_call | solution.py:171
  (9 shorter events, 0.1 us)
Async XLA Ops:
  0.6 0.7 copy-start.5
  1.3 0.9 %copy-start = (s32[1,1,1,16,4096]{4,3,2,1,0:T(8,128)S(1)}, s32[1,1,1,16,4096]{4,3,2,1,0:T(8,128)}, u32[]{:S(2)}) copy-start(s32[1,1,1,16,4096]{4,3,2,1,0:T(8,128)} %param.6) | copy-start | bytes 786436
  2.2 0.9 %copy-start.6 = (f32[1,1,1,16,4096]{4,3,2,1,0:T(8,128)S(1)}, f32[1,1,1,16,4096]{4,3,2,1,0:T(8,128)}, u32[]{:S(2)}) copy-start(f32[1,1,1,16,4096]{4,3,2,1,0:T(8,128)} %param.7) | copy-start | bytes 786436
  3.2 4.9 %copy-start.1 = (s32[1,1,1,16,4096]{4,3,2,1,0:T(8,128)S(1)}, s32[1,1,1,16,4096]{4,3,2,1,0:T(8,128)}, u32[]{:S(2)}) copy-start(s32[1,1,1,16,4096]{4,3,2,1,0:T(8,128)} %param.6) | copy-start | bytes 786436
  7.3 5.0 %collective-permute-start = (f32[8,16,512]{2,1,0:T(8,128)S(1)}, f32[8,16,512]{2,1,0:T(8,128)S(1)}, u32[]{:S(2)}, u32[]{:S(2)}) collective-permute-start(f32[8,16,512]{2,1,0:T(8,128)S(1)} %deposit.3), channel_id=1, source_target_pairs={{0,16},{16,0},{32,48},{48,32},{64,80},{80,64},{96,112},{112,96},{1... | collective-permute-start | bytes 786440 | tf_op jit(solution)/shard_map/ppermute | solution.py:193
  12.4 20.4 %copy-start.2 = (s32[16,512]{1,0:T(8,128)S(1)}, s32[16,512]{1,0:T(8,128)}, u32[]{:S(2)}) copy-start(s32[16,512]{1,0:T(8,128)} %materials_ref.1) | copy-start | bytes 98308
  12.4 20.4 %copy-start.3 = (f32[16,512]{1,0:T(8,128)S(1)}, f32[16,512]{1,0:T(8,128)}, u32[]{:S(2)}) copy-start(f32[16,512]{1,0:T(8,128)} %target_ref.1) | copy-start | bytes 98308
  12.4 20.4 %copy-start.4 = (f32[4]{0:T(128)S(1)}, f32[4]{0:T(128)}, u32[]{:S(2)}) copy-start(f32[4]{0:T(128)} %coef_ref.1) | copy-start | bytes 52
  33.3 5.3 %collective-permute-start.1 = (f32[3,16,128]{2,1,0:T(8,128)S(1)}, f32[3,16,128]{2,1,0:T(8,128)S(1)}, u32[]{:S(2)}, u32[]{:S(2)}) collective-permute-start(f32[3,16,128]{2,1,0:T(8,128)S(1)} %get-tuple-element.11), channel_id=1, source_target_pairs={{0,1},{1,2},{2,3},{4,5},{5,6},{6,7},{8,9},{9,10},{10,11},{12,13},{... | collective-permute-start | bytes 73736 | tf_op jit(solution)/shard_map/ppermute | solution.py:182
  36.2 4.6 %collective-permute-start.2 = (f32[3,16,128]{2,1,0:T(8,128)S(1)}, f32[3,16,128]{2,1,0:T(8,128)S(1)}, u32[]{:S(2)}, u32[]{:S(2)}) collective-permute-start(f32[3,16,128]{2,1,0:T(8,128)S(1)} %get-tuple-element.12), channel_id=1, source_target_pairs={{1,0},{2,1},{3,2},{5,4},{6,5},{7,6},{9,8},{10,9},{11,10},{13,12},{... | collective-permute-start | bytes 73736 | tf_op jit(solution)/shard_map/ppermute | solution.py:182
  40.8 8.3 %collective-permute-start.3 = (f32[16,768]{1,0:T(8,128)S(1)}, f32[16,768]{1,0:T(8,128)S(1)}, u32[]{:S(2)}, u32[]{:S(2)}) collective-permute-start(f32[16,768]{1,0:T(8,128)S(1)} %get-tuple-element.14), channel_id=1, source_target_pairs={{0,4},{4,8},{8,12},{12,16},{16,20},{20,24},{24,28},{28,32},{32,36}... | collective-permute-start | bytes 147464 | tf_op jit(solution)/shard_map/ppermute | solution.py:182
  44.0 6.3 %collective-permute-start.4 = (f32[16,768]{1,0:T(8,128)S(1)}, f32[16,768]{1,0:T(8,128)S(1)}, u32[]{:S(2)}, u32[]{:S(2)}) collective-permute-start(f32[16,768]{1,0:T(8,128)S(1)} %get-tuple-element.15), channel_id=1, source_target_pairs={{4,0},{8,4},{12,8},{16,12},{20,16},{24,20},{28,24},{32,28},{36,32}... | collective-permute-start | bytes 147464 | tf_op jit(solution)/shard_map/ppermute | solution.py:182

commit v2 on v1

v2 whole, which is shorter than its diff:
```python
import functools

import jax
import jax.numpy as jnp
from jax import lax
from jax.experimental import pallas as pl
from jax.experimental.pallas import tpu as pltpu
from jax.sharding import PartitionSpec as P

STEPS = 3
SPAN = 512
LANES = 128
VMEM = pl.BlockSpec(memory_space=pltpu.VMEM)
SMEM = pl.BlockSpec(memory_space=pltpu.SMEM)
PARAMS = pltpu.CompilerParams(vmem_limit_bytes=32 << 20)
F32 = jnp.float32
BF16 = jnp.bfloat16


def f32(*shape):
    return jax.ShapeDtypeStruct(shape, F32)


def rows_of(value, kind):
    return jnp.broadcast_to(value, (16, value.shape[1])).astype(kind)


def hot(index, groups, filled):
    width = index.shape[1]
    ids = rows_of(index, jnp.int16)
    iota = lax.broadcasted_iota(jnp.int16, (16, width), 0)
    masks = [ids == iota + jnp.int16(16 * g) for g in range(groups)]
    zero = jnp.bfloat16(0)
    return [jnp.concatenate([jnp.where(m, f, zero) for m in masks], axis=0) for f in filled]


COST = pl.CostEstimate(flops=1 << 30, bytes_accessed=1 << 18, transcendentals=0)


def split(cell):
    return ((cell >> 7) & 3) * 16 + (cell >> 9), cell & 127


def deposit_kernel(side, info_ref, counts_ref, cells_ref, dose_ref, out_ref):
    core = info_ref[0] ^ side
    slots = cells_ref.shape[1]

    def strip(j, carry):
        o = 2 * j + core
        count = counts_ref[o]
        total = jnp.zeros((2 * 64, LANES), F32)
        for k in range(0, slots, SPAN):
            cell = cells_ref[pl.ds(o, 1), k : k + SPAN]
            slot = lax.broadcasted_iota(jnp.int32, (1, SPAN), 1) + k
            dose = jnp.where(slot < count, dose_ref[pl.ds(o, 1), k : k + SPAN], 0.0)
            high = dose.astype(BF16).astype(F32)
            chunk, lane = split(cell)
            rows = hot(chunk, 4, [rows_of(high, BF16), rows_of(dose - high, BF16)])
            (cols,) = hot(lane, 8, [jnp.bfloat16(1)])
            total = total + lax.dot_general(
                jnp.concatenate(rows, axis=0),
                cols,
                (((1,), (1,)), ((), ())),
                preferred_element_type=F32,
            )
        both = total[:64] + total[64:]
        for q in range(4):
            out_ref[j, :, q * LANES : (q + 1) * LANES] = both[16 * q : 16 * q + 16]
        return carry

    lax.fori_loop(0, out_ref.shape[0], strip, 0, unroll=4)


def deposit(side, info, counts, cells, dose):
    return pl.pallas_call(
        functools.partial(deposit_kernel, side),
        out_shape=f32(8, 16, 512),
        in_specs=[SMEM, SMEM, VMEM, VMEM],
        out_specs=VMEM,
        compiler_params=PARAMS,
        cost_estimate=pl.CostEstimate(flops=1 << 30, bytes_accessed=1 << 19, transcendentals=0),
        name="deposit",
    )(info, counts, cells, dose)


def gather_kernel(info_ref, coef_ref, parts_ref, materials_ref, target_ref, *outs):
    mid_ref, first_ref, second_ref = outs
    even = info_ref[1] == 0
    strip = parts_ref[0]
    for z in range(1, parts_ref.shape[0]):
        strip = strip + parts_ref[z]
    materials = materials_ref[...]
    spread = jnp.zeros(materials.shape, F32)
    for index in range(coef_ref.shape[0]):
        spread = jnp.where(materials == index, coef_ref[index], spread)
    for i, value in enumerate((strip, spread, target_ref[...])):
        mid_ref[i] = value
        left, right = value[:, :LANES], value[:, -LANES:]
        first_ref[i] = jnp.where(even, right, left)
        second_ref[i] = jnp.where(even, left, right)


def widen_kernel(info_ref, mid_ref, first_ref, second_ref, wide_ref, send_ref, later_ref):
    even, even_y = info_ref[1] == 0, info_ref[2] == 0
    near = lax.broadcasted_iota(jnp.int32, (16, LANES), 1) < LANES // 2
    for i in range(3):
        first, second = first_ref[i], second_ref[i]
        left = jnp.where(even, second, first)
        right = jnp.where(even, first, second)
        wide = jnp.concatenate([mid_ref[i], jnp.where(near, right, left)], axis=1)
        wide_ref[i] = wide
        if i == 0:
            top, bottom = wide[:8], wide[8:]
        elif i == 1:
            top, bottom = jnp.concatenate([top, wide[:5]]), jnp.concatenate([bottom, wide[11:]])
        else:
            top, bottom = jnp.concatenate([top, wide[:3]]), jnp.concatenate([bottom, wide[13:]])
    send_ref[...] = jnp.where(even_y, bottom, top)
    later_ref[...] = jnp.where(even_y, top, bottom)


def neighbours(field):
    height, width = field.shape
    return (
        pltpu.roll(field, 1, 0)
        + pltpu.roll(field, height - 1, 0)
        + pltpu.roll(field, 1, 1)
        + pltpu.roll(field, width - 1, 1)
    )


def blur_kernel(info_ref, wide_ref, first_ref, second_ref, exposure_ref, adjoint_ref):
    even = info_ref[2] == 0
    first, second = first_ref[...], second_ref[...]
    above, below = jnp.where(even, second, first), jnp.where(even, first, second)
    width = wide_ref.shape[2]
    blank = lambda rows: jnp.zeros((rows, width), F32)
    field = jnp.concatenate([above[:8], wide_ref[0], below[:8]], axis=0)
    spread = jnp.concatenate(
        [blank(3), above[8:13], wide_ref[1], below[8:13], blank(3)], axis=0
    )
    target = jnp.concatenate(
        [blank(5), above[13:], wide_ref[2], below[13:], blank(5)], axis=0
    )
    for step in range(STEPS):
        field = field + spread * (neighbours(field) - 4.0 * field)
    exposure_ref[...] = field[8:24, :-LANES]
    field = field - target
    for step in range(STEPS):
        weighted = spread * field
        field = field + neighbours(weighted) - 4.0 * weighted
    for q in range(4):
        for z in range(adjoint_ref.shape[0]):
            adjoint_ref[z, 16 * q : 16 * q + 16] = field[8:24, q * LANES : (q + 1) * LANES]


def pick_strips(core, counts_ref, cells_ref, table_ref, store):
    slots = cells_ref.shape[1]

    def strip(z, carry):
        o = 2 * z + core
        table = table_ref[z]
        high = table.astype(BF16)
        low = (table - high.astype(F32)).astype(BF16)
        both = jnp.concatenate([high, low], axis=0)
        count = counts_ref[o]
        for k in range(0, slots, SPAN):
            chunk, lane = split(cells_ref[pl.ds(o, 1), k : k + SPAN])
            (cols,) = hot(lane, 8, [jnp.bfloat16(1)])
            across = jnp.dot(both, cols, preferred_element_type=F32)
            across = across[:64] + across[64:]
            iota = lax.broadcasted_iota(jnp.int32, (8, SPAN), 0)
            chosen = jnp.broadcast_to(chunk, (8, SPAN))
            value = jnp.zeros((8, SPAN), F32)
            for g in range(8):
                value = jnp.where(chosen == iota + 8 * g, across[8 * g : 8 * g + 8], value)
            value = jnp.sum(value, axis=0, keepdims=True)
            slot = lax.broadcasted_iota(jnp.int32, (1, SPAN), 1) + k
            store(z, o, k, jnp.where(slot < count, value, 0.0))
        return carry

    lax.fori_loop(0, table_ref.shape[0], strip, 0, unroll=4)


def pick_kernel(info_ref, counts_ref, cells_ref, table_ref, out_ref):
    def store(z, o, k, value):
        out_ref[pl.ds(z, 1), k : k + SPAN] = value

    pick_strips(info_ref[0], counts_ref, cells_ref, table_ref, store)


def last_kernel(info_ref, counts_ref, cells_ref, table_ref, own_ref, out_ref):
    def store(z, o, k, value):
        out_ref[pl.ds(o, 1), k : k + SPAN] = value

    pick_strips(1 - info_ref[0], counts_ref, cells_ref, table_ref, store)
    for z in range(own_ref.shape[0]):
        out_ref[pl.ds(2 * z + info_ref[0], 1), :] = own_ref[z : z + 1, :]


def pick(info, counts, cells, table, own=None):
    last = own is not None
    return pl.pallas_call(
        last_kernel if last else pick_kernel,
        out_shape=f32(cells.shape[0] if last else table.shape[0], cells.shape[1]),
        in_specs=[SMEM, SMEM] + [VMEM] * (3 if last else 2),
        out_specs=VMEM,
        compiler_params=PARAMS,
        cost_estimate=COST,
        name="pick_last" if last else "pick",
    )(info, counts, cells, table, *([own] if last else []))


def swap(value, axes, bits):
    count = lax.axis_size(axes)
    return lax.ppermute(value, axes, [(i, i ^ bits) for i in range(count)])


def swap_later(value, axes):
    count = lax.axis_size(axes)
    pairs = [(i, i + 1) for i in range(1, count - 1, 2)]
    return lax.ppermute(value, axes, pairs + [(j, i) for i, j in pairs])


def local(shot_cells, shot_dose, shot_counts, materials, coefficients, target):
    cells, dose, counts = shot_cells[0, 0, 0], shot_dose[0, 0, 0], shot_counts[0, 0, 0]
    shots = lax.axis_size("shots")
    info = jnp.stack(
        [lax.axis_index("shots") % 2, lax.axis_index("gx") % 2, lax.axis_index("gy") % 2]
    ).astype(jnp.int32)
    lines = [[2 * z + c for z in range(shots // 2)] for c in range(2)]

    def exchange(value):
        return lax.all_to_all(value, "shots", 0, 0, axis_index_groups=lines, tiled=True)

    away = swap(deposit(1, info, counts, cells, dose), "shots", 1)
    parts = exchange(deposit(0, info, counts, cells, dose) + away)

    mid, first, second = pl.pallas_call(
        gather_kernel,
        out_shape=(f32(3, 16, 512), f32(3, 16, LANES), f32(3, 16, LANES)),
        in_specs=[SMEM] * 2 + [VMEM] * 3,
        out_specs=(VMEM,) * 3,
        compiler_params=PARAMS,
        name="gather",
    )(info, coefficients, parts, materials, target)
    wide, first, second = pl.pallas_call(
        widen_kernel,
        out_shape=(f32(3, 16, 640), f32(16, 640), f32(16, 640)),
        in_specs=[SMEM] + [VMEM] * 3,
        out_specs=(VMEM,) * 3,
        compiler_params=PARAMS,
        name="widen",
    )(info, mid, swap(first, "gx", 1), swap_later(second, "gx"))
    rows = ("shots", "gy")
    exposure, adjoint = pl.pallas_call(
        blur_kernel,
        out_shape=(f32(16, 512), f32(shots // 2, 64, LANES)),
        in_specs=[SMEM] + [VMEM] * 3,
        out_specs=(VMEM,) * 2,
        compiler_params=PARAMS,
        name="blur",
    )(info, wide, swap(first, rows, 1), swap_later(second, rows))

    table = exchange(adjoint)
    other = swap(table, "shots", 1)
    shot_grad = pick(info, counts, cells, other, pick(info, counts, cells, table))
    return (exposure, shot_grad[None, None, None])


def solution(mesh):
    placed = (
        P("shots", "gy", "gx", None, None),
        P("shots", "gy", "gx", None, None),
        P("shots", "gy", "gx", None),
        P(("shots", "gy"), "gx"),
        P(),
        P(("shots", "gy"), "gx"),
    )
    return jax.shard_map(
        local,
        mesh=mesh,
        in_specs=placed,
        out_specs=(P(("shots", "gy"), "gx"), P("shots", "gy", "gx", None, None)),
        check_vma=False,
    )
```

time: 79 us -> 70.8 us (0.90); the launches traced: 77.5 us -> 70.4 us
  blocking collectives: 38.2 us -> 32.4 us
  Pallas kernels: 18.2 us -> 15.7 us
  waiting for transfers between devices: 3.3 us -> 4.3 us
    all_gather x1 -> x0, blocking collectives: 17.9 us -> none  [local(): table = lax.all_gather(adjoint, 'shots', axis=0, tiled=True)]
    all_to_all x1 -> x2, blocking collectives: 20.3 us -> 32.4 us  [exchange(): lax.all_to_all(value, 'shots', 0, 0, axis_index_groups=lines, tiled=True)]
    pallas_call x5 -> x6, Pallas kernels: 17.7 us -> 15.2 us  [the longest x2 6.88 us: pick(): pl.pallas_call(last_kernel if last else pick_kernel, out_shape=f32(cells....]
    ppermute x5 -> x6, waiting for transfers between devices: 3.3 us -> 4.3 us  [the longest x2 4.29 us: swap_later(): return lax.ppermute(value, axes, pairs + [(j, i) for i, j in pairs])]
    ppermute x5 -> x6, starting transfers between devices: 14.4 us -> 14.5 us  [the longest x2 7.76 us: swap_later(): return lax.ppermute(value, axes, pairs + [(j, i) for i, j in pairs])]
  transfers between devices with their start and end apart: 5 -> 6, of which waited for: 2 -> 2; matrix products, arithmetic and copies ran while one was open for 0% -> 0% of each run, Pallas kernels for 5% -> 9%
where the time goes in v2:
time: 70.8 us; the launch traced here: 70.4 us
  blocking collectives  32.4 us (46%)
  Pallas kernels  15.7 us (22%)
  starting transfers between devices  14.5 us (20%)
  waiting for transfers between devices  4.3 us (6%)
  local copies, waits for them, and re-layouts  2.58 us (4%)
  between operations  0.78 us (1%)
    all_to_all x2, blocking collectives, exchange(): lax.all_to_all(value, 'shots', 0, 0, axis_index_groups=lines, tiled=True)  32.4 us
    ppermute x2, starting transfers between devices, swap_later(): return lax.ppermute(value, axes, pairs + [(j, i) for i, j in pairs])  7.76 us
    pallas_call x2, Pallas kernels, pick(): pl.pallas_call(last_kernel if last else pick_kernel, out_shape=f32(cells....  6.88 us
    ppermute x4, starting transfers between devices, swap(): return lax.ppermute(value, axes, [(i, i ^ bits) for i in range(count)])  6.7 us
    pallas_call x2, Pallas kernels, deposit(): pl.pallas_call(functools.partial(deposit_kernel, side), out_shape=f32(8,...  6.13 us
    ppermute x2, waiting for transfers between devices, swap_later(): return lax.ppermute(value, axes, pairs + [(j, i) for i, j in pairs])  4.29 us
    unnamed x14, local copies, waits for them, and re-layouts  2.58 us
    pallas_call x1, Pallas kernels, local(): pl.pallas_call(blur_kernel, out_shape=(f32(16, 512), f32(shots // 2, 64,...  1.61 us
  transfers between devices with their start and end apart: 6, of which 2 were waited for; matrix products, arithmetic and copies ran while one was open for 0% of the time, Pallas kernels for 9%

profile of v2, /device:TPU:5, one launch (start us, length us, event | category | flops | bytes accessed | tf_op | source)
XLA Modules:
  0.0 70.4 jit_solution(16647006735634582169)
XLA Ops:
  0.7 0.1 pad_add_fusion.info_ref
  0.7 0.7 copy-done.6
  1.4 0.9 %copy-done.3 = f32[1,1,1,16,4096]{4,3,2,1,0:T(8,128)S(1)} copy-done((f32[1,1,1,16,4096]{4,3,2,1,0:T(8,128)S(1)}, f32[1,1,1,16,4096]{4,3,2,1,0:T(8,128)}, u32[]{:S(2)}) %copy-start.3) | copy-done | bytes 262168
  2.3 0.9 %copy-done.4 = s32[1,1,1,16,4096]{4,3,2,1,0:T(8,128)S(1)} copy-done((s32[1,1,1,16,4096]{4,3,2,1,0:T(8,128)S(1)}, s32[1,1,1,16,4096]{4,3,2,1,0:T(8,128)}, u32[]{:S(2)}) %copy-start.4) | copy-done | bytes 262168
  3.3 3.1 %deposit.3 = f32[8,16,512]{2,1,0:T(8,128)S(1)} custom-call(s32[3]{0:T(128)S(1)} %pad_add_fusion.info_ref, s32[16]{0:T(128)S(1)} %bitcast.13, s32[16,4096]{1,0:T(8,128)S(1)} %bitcast.9, f32[16,4096]{1,0:T(8,128)S(1)} %bitcast.7), custom_call_target="tpu_custom_call" | custom-call | flops 1073741824 | bytes 524288 | tf_op jit(solution)/shard_map/deposit/pallas_call | solution.py:75
  6.4 0.8 %collective-permute-start = (f32[8,16,512]{2,1,0:T(8,128)S(1)}, f32[8,16,512]{2,1,0:T(8,128)S(1)}, u32[]{:S(2)}, u32[]{:S(2)}) collective-permute-start(f32[8,16,512]{2,1,0:T(8,128)S(1)} %deposit.3), channel_id=1, source_target_pairs={{0,16},{16,0},{32,48},{48,32},{64,80},{80,64},{96,112},{112,96},{1... | collective-permute-start | bytes 786440 | tf_op jit(solution)/shard_map/ppermute | solution.py:216
  7.1 3.1 %deposit.2 = f32[8,16,512]{2,1,0:T(8,128)S(1)} custom-call(s32[3]{0:T(128)S(1)} %pad_add_fusion.info_ref, s32[16]{0:T(128)S(1)} %bitcast.14, s32[16,4096]{1,0:T(8,128)S(1)} %bitcast.10, f32[16,4096]{1,0:T(8,128)S(1)} %bitcast.8), custom_call_target="tpu_custom_call" | custom-call | flops 1073741824 | bytes 524288 | tf_op jit(solution)/shard_map/deposit/pallas_call | solution.py:75
  10.2 0.0 copy-start
  10.3 0.0 copy-start.1
  10.3 0.0 copy-start.2
  10.3 20.5 %all_to_all.10.parts_ref = f32[8,16,512]{2,1,0:T(8,128)S(1)} all-to-all(f32[8,16,512]{2,1,0:T(8,128)S(1)} %add.16), channel_id=1, replica_groups={{0,32,64,96,128,160,192,224},{16,48,80,112,144,176,208,240},{1,33,65,97..., dimensions={0} | all-to-all | bytes 524288 | tf_op jit(solution)/shard_map/all_to_all | solution.py:234
  30.8 0.6 gather.1
  31.4 1.0 %collective-permute-start.1 = (f32[3,16,128]{2,1,0:T(8,128)S(1)}, f32[3,16,128]{2,1,0:T(8,128)S(1)}, u32[]{:S(2)}, u32[]{:S(2)}) collective-permute-start(f32[3,16,128]{2,1,0:T(8,128)S(1)} %get-tuple-element.11), channel_id=1, source_target_pairs={{0,1},{1,0},{2,3},{3,2},{4,5},{5,4},{6,7},{7,6},{8,9},{9,8},{10,11... | collective-permute-start | bytes 73736 | tf_op jit(solution)/shard_map/ppermute | solution.py:216
  32.4 1.9 %collective-permute-start.2 = (f32[3,16,128]{2,1,0:T(8,128)S(1)}, f32[3,16,128]{2,1,0:T(8,128)S(1)}, u32[]{:S(2)}, u32[]{:S(2)}) collective-permute-start(f32[3,16,128]{2,1,0:T(8,128)S(1)} %get-tuple-element.12), channel_id=1, source_target_pairs={{1,2},{2,1},{5,6},{6,5},{9,10},{10,9},{13,14},{14,13},{17,18},{18,... | collective-permute-start | bytes 73736 | tf_op jit(solution)/shard_map/ppermute | solution.py:222
  34.3 2.6 %collective-permute-done.2.second_ref = f32[3,16,128]{2,1,0:T(8,128)S(1)} collective-permute-done((f32[3,16,128]{2,1,0:T(8,128)S(1)}, f32[3,16,128]{2,1,0:T(8,128)S(1)}, u32[]{:S(2)}, u32[]{:S(2)}) %collective-permute-start.2) | collective-permute-done | bytes 24608 | tf_op jit(solution)/shard_map/ppermute | solution.py:222
  36.9 0.6 widen.1
  37.5 1.4 %collective-permute-start.3 = (f32[16,640]{1,0:T(8,128)S(1)}, f32[16,640]{1,0:T(8,128)S(1)}, u32[]{:S(2)}, u32[]{:S(2)}) collective-permute-start(f32[16,640]{1,0:T(8,128)S(1)} %get-tuple-element.14), channel_id=1, source_target_pairs={{0,4},{4,0},{8,12},{12,8},{16,20},{20,16},{24,28},{28,24},{32,36},... | collective-permute-start | bytes 122888 | tf_op jit(solution)/shard_map/ppermute | solution.py:216
  38.9 5.9 %collective-permute-start.4 = (f32[16,640]{1,0:T(8,128)S(1)}, f32[16,640]{1,0:T(8,128)S(1)}, u32[]{:S(2)}, u32[]{:S(2)}) collective-permute-start(f32[16,640]{1,0:T(8,128)S(1)} %get-tuple-element.15), channel_id=1, source_target_pairs={{4,8},{12,16},{20,24},{28,32},{36,40},{44,48},{52,56},{60,64},{68,... | collective-permute-start | bytes 122888 | tf_op jit(solution)/shard_map/ppermute | solution.py:222
  44.7 1.7 %collective-permute-done.4.second_ref = f32[16,640]{1,0:T(8,128)S(1)} collective-permute-done((f32[16,640]{1,0:T(8,128)S(1)}, f32[16,640]{1,0:T(8,128)S(1)}, u32[]{:S(2)}, u32[]{:S(2)}) %collective-permute-start.4) | collective-permute-done | bytes 40992 | tf_op jit(solution)/shard_map/ppermute | solution.py:222
  46.4 1.6 %blur.1 = (f32[16,512]{1,0:T(8,128)}, f32[8,64,128]{2,1,0:T(8,128)S(1)}) custom-call(s32[3]{0:T(128)S(1)} %pad_add_fusion.info_ref, f32[3,16,640]{2,1,0:T(8,128)S(1)} %get-tuple-element.13.wide_ref, f32[16,640]{1,0:T(8,128)S(1)} %collective-permute-done.3.first_ref, f32[16,640]{1,0:T(8,128)S(1)} %collective-permute-done.4.second_ref), custom_call_target="tpu_custom_call" | custom-call | tf_op jit(solution)/shard_map/blur/pallas_call | solution.py:256
  48.0 12.0 %all_to_all.11.table_ref = f32[8,64,128]{2,1,0:T(8,128)S(1)} all-to-all(f32[8,64,128]{2,1,0:T(8,128)S(1)} %get-tuple-element.17), channel_id=1, replica_groups={{0,32,64,96,128,160,192,224},{16,48,80,112,144,176,208,240},{1,33,65,97..., dimensions={0} | all-to-all | bytes 524288 | tf_op jit(solution)/shard_map/all_to_all | solution.py:234
  60.0 3.6 %collective-permute-start.5 = (f32[8,64,128]{2,1,0:T(8,128)S(1)}, f32[8,64,128]{2,1,0:T(8,128)S(1)}, u32[]{:S(2)}, u32[]{:S(2)}) collective-permute-start(f32[8,64,128]{2,1,0:T(8,128)S(1)} %all_to_all.11.table_ref), channel_id=1, source_target_pairs={{0,16},{16,0},{32,48},{48,32},{64,80},{80,64},{96,112},{112,96},{1... | collective-permute-start | bytes 786440 | tf_op jit(solution)/shard_map/ppermute | solution.py:216
  63.5 3.1 %pick.1.own_ref = f32[8,4096]{1,0:T(8,128)S(1)} custom-call(s32[3]{0:T(128)S(1)} %pad_add_fusion.info_ref, s32[16]{0:T(128)S(1)} %bitcast.15, s32[16,4096]{1,0:T(8,128)S(1)} %bitcast.11, f32[8,64,128]{2,1,0:T(8,128)S(1)} %all_to_all.11.table_ref), custom_call_target="tpu_custom_call" | custom-call | flops 1073741824 | bytes 262144 | tf_op jit(solution)/shard_map/pick/pallas_call | solution.py:203
  66.6 3.8 %pick_last.1 = f32[16,4096]{1,0:T(8,128)} custom-call(s32[3]{0:T(128)S(1)} %pad_add_fusion.info_ref, s32[16]{0:T(128)S(1)} %bitcast.16, s32[16,4096]{1,0:T(8,128)S(1)} %bitcast.12, f32[8,64,128]{2,1,0:T(8,128)S(1)} %collective-permute-done.5.table_ref, f32[8,4096]{1,0:T(8,128)S(1)} %pick.1.own_ref), custom_call_target="tpu_custom_call" | custom-call | flops 1073741824 | bytes 262144 | tf_op jit(solution)/shard_map/pick_last/pallas_call | solution.py:203
  (13 shorter events, 0.1 us)
Async XLA Ops:
  0.7 0.7 copy-start.6
  1.4 0.9 %copy-start.3 = (f32[1,1,1,16,4096]{4,3,2,1,0:T(8,128)S(1)}, f32[1,1,1,16,4096]{4,3,2,1,0:T(8,128)}, u32[]{:S(2)}) copy-start(f32[1,1,1,16,4096]{4,3,2,1,0:T(8,128)} %param.7) | copy-start | bytes 786436
  2.3 0.9 %copy-start.4 = (s32[1,1,1,16,4096]{4,3,2,1,0:T(8,128)S(1)}, s32[1,1,1,16,4096]{4,3,2,1,0:T(8,128)}, u32[]{:S(2)}) copy-start(s32[1,1,1,16,4096]{4,3,2,1,0:T(8,128)} %param.6) | copy-start | bytes 786436
  6.4 3.8 %collective-permute-start = (f32[8,16,512]{2,1,0:T(8,128)S(1)}, f32[8,16,512]{2,1,0:T(8,128)S(1)}, u32[]{:S(2)}, u32[]{:S(2)}) collective-permute-start(f32[8,16,512]{2,1,0:T(8,128)S(1)} %deposit.3), channel_id=1, source_target_pairs={{0,16},{16,0},{32,48},{48,32},{64,80},{80,64},{96,112},{112,96},{1... | collective-permute-start | bytes 786440 | tf_op jit(solution)/shard_map/ppermute | solution.py:216
  10.2 20.5 %copy-start = (s32[16,512]{1,0:T(8,128)S(1)}, s32[16,512]{1,0:T(8,128)}, u32[]{:S(2)}) copy-start(s32[16,512]{1,0:T(8,128)} %materials_ref.1) | copy-start | bytes 98308
  10.3 20.5 %copy-start.1 = (f32[16,512]{1,0:T(8,128)S(1)}, f32[16,512]{1,0:T(8,128)}, u32[]{:S(2)}) copy-start(f32[16,512]{1,0:T(8,128)} %target_ref.1) | copy-start | bytes 98308
  10.3 20.5 %copy-start.2 = (f32[4]{0:T(128)S(1)}, f32[4]{0:T(128)}, u32[]{:S(2)}) copy-start(f32[4]{0:T(128)} %coef_ref.1) | copy-start | bytes 52
  31.4 2.9 %collective-permute-start.1 = (f32[3,16,128]{2,1,0:T(8,128)S(1)}, f32[3,16,128]{2,1,0:T(8,128)S(1)}, u32[]{:S(2)}, u32[]{:S(2)}) collective-permute-start(f32[3,16,128]{2,1,0:T(8,128)S(1)} %get-tuple-element.11), channel_id=1, source_target_pairs={{0,1},{1,0},{2,3},{3,2},{4,5},{5,4},{6,7},{7,6},{8,9},{9,8},{10,11... | collective-permute-start | bytes 73736 | tf_op jit(solution)/shard_map/ppermute | solution.py:216
  32.4 4.6 %collective-permute-start.2 = (f32[3,16,128]{2,1,0:T(8,128)S(1)}, f32[3,16,128]{2,1,0:T(8,128)S(1)}, u32[]{:S(2)}, u32[]{:S(2)}) collective-permute-start(f32[3,16,128]{2,1,0:T(8,128)S(1)} %get-tuple-element.12), channel_id=1, source_target_pairs={{1,2},{2,1},{5,6},{6,5},{9,10},{10,9},{13,14},{14,13},{17,18},{18,... | collective-permute-start | bytes 73736 | tf_op jit(solution)/shard_map/ppermute | solution.py:222
  37.5 7.2 %collective-permute-start.3 = (f32[16,640]{1,0:T(8,128)S(1)}, f32[16,640]{1,0:T(8,128)S(1)}, u32[]{:S(2)}, u32[]{:S(2)}) collective-permute-start(f32[16,640]{1,0:T(8,128)S(1)} %get-tuple-element.14), channel_id=1, source_target_pairs={{0,4},{4,0},{8,12},{12,8},{16,20},{20,16},{24,28},{28,24},{32,36},... | collective-permute-start | bytes 122888 | tf_op jit(solution)/shard_map/ppermute | solution.py:216
  38.9 7.5 %collective-permute-start.4 = (f32[16,640]{1,0:T(8,128)S(1)}, f32[16,640]{1,0:T(8,128)S(1)}, u32[]{:S(2)}, u32[]{:S(2)}) collective-permute-start(f32[16,640]{1,0:T(8,128)S(1)} %get-tuple-element.15), channel_id=1, source_target_pairs={{4,8},{12,16},{20,24},{28,32},{36,40},{44,48},{52,56},{60,64},{68,... | collective-permute-start | bytes 122888 | tf_op jit(solution)/shard_map/ppermute | solution.py:222
  48.0 15.5 %copy-start.5 = (s32[1,1,1,16,4096]{4,3,2,1,0:T(8,128)S(1)}, s32[1,1,1,16,4096]{4,3,2,1,0:T(8,128)}, u32[]{:S(2)}) copy-start(s32[1,1,1,16,4096]{4,3,2,1,0:T(8,128)} %param.6) | copy-start | bytes 786436
  60.0 6.6 %collective-permute-start.5 = (f32[8,64,128]{2,1,0:T(8,128)S(1)}, f32[8,64,128]{2,1,0:T(8,128)S(1)}, u32[]{:S(2)}, u32[]{:S(2)}) collective-permute-start(f32[8,64,128]{2,1,0:T(8,128)S(1)} %all_to_all.11.table_ref), channel_id=1, source_target_pairs={{0,16},{16,0},{32,48},{48,32},{64,80},{80,64},{96,112},{112,96},{1... | collective-permute-start | bytes 786440 | tf_op jit(solution)/shard_map/ppermute | solution.py:216

commit v3 on v2

--- a/solution.py
+++ b/solution.py
@@ -11,7 +11,7 @@
 SPAN = 512
 LANES = 128
 VMEM = pl.BlockSpec(memory_space=pltpu.VMEM)
-SMEM = pl.BlockSpec(memory_space=pltpu.SMEM)
+HBM = pl.BlockSpec(memory_space=pltpu.HBM)
 PARAMS = pltpu.CompilerParams(vmem_limit_bytes=32 << 20)
 F32 = jnp.float32
 BF16 = jnp.bfloat16
@@ -41,18 +41,25 @@
     return ((cell >> 7) & 3) * 16 + (cell >> 9), cell & 127
 
 
-def deposit_kernel(side, info_ref, counts_ref, cells_ref, dose_ref, out_ref):
-    core = info_ref[0] ^ side
+def own_core():
+    return lax.axis_index("shots") % 2
+
+
+def alive(counts_ref, strip, k):
+    count = jnp.concatenate([counts_ref[pl.ds(strip, 1), :]] * (SPAN // LANES), axis=1)
+    return lax.broadcasted_iota(jnp.int32, (1, SPAN), 1) + k < count
+
+
+def deposit_kernel(side, counts_ref, cells_ref, dose_ref, out_ref):
+    core = own_core() ^ side
     slots = cells_ref.shape[1]
 
     def strip(j, carry):
         o = 2 * j + core
-        count = counts_ref[o]
         total = jnp.zeros((2 * 64, LANES), F32)
         for k in range(0, slots, SPAN):
             cell = cells_ref[pl.ds(o, 1), k : k + SPAN]
-            slot = lax.broadcasted_iota(jnp.int32, (1, SPAN), 1) + k
-            dose = jnp.where(slot < count, dose_ref[pl.ds(o, 1), k : k + SPAN], 0.0)
+            dose = jnp.where(alive(counts_ref, o, k), dose_ref[pl.ds(o, 1), k : k + SPAN], 0.0)
             high = dose.astype(BF16).astype(F32)
             chunk, lane = split(cell)
             rows = hot(chunk, 4, [rows_of(high, BF16), rows_of(dose - high, BF16)])
@@ -71,37 +78,79 @@
     lax.fori_loop(0, out_ref.shape[0], strip, 0, unroll=4)
 
 
-def deposit(side, info, counts, cells, dose):
+def first_kernel(*refs):
+    sources, (out_ref, counts_ref, cells, dose, spread_ref) = refs[:5], refs[5:10]
+    counts, materials, coefs, sems = refs[10:]
+    targets = (counts, coefs, cells, dose, materials)
+    copies = [
+        pltpu.make_async_copy(source, target, sems.at[i])
+        for i, (source, target) in enumerate(zip(sources, targets))
+    ]
+    for copy in copies:
+        copy.start()
+    for copy in copies:
+        copy.wait()
+    for o in range(counts_ref.shape[0]):
+        counts_ref[o : o + 1, :] = jnp.full((1, LANES), counts[o], jnp.int32)
+    spread = jnp.zeros(materials.shape, F32)
+    for index in range(coefs.shape[0]):
+        spread = jnp.where(materials[...] == index, coefs[index], spread)
+    spread_ref[...] = spread
+    deposit_kernel(1, counts_ref, cells, dose, out_ref)
+
+
+def deposit_first(counts, coefficients, cells, dose, materials):
+    inputs = (counts, coefficients, cells, dose, materials)
+    same = lambda value: jax.ShapeDtypeStruct(value.shape, value.dtype)
     return pl.pallas_call(
-        functools.partial(deposit_kernel, side),
+        first_kernel,
+        out_shape=(
+            f32(8, 16, 512),
+            jax.ShapeDtypeStruct((counts.shape[0], LANES), jnp.int32),
+            same(cells),
+            same(dose),
+            f32(*materials.shape),
+        ),
+        in_specs=[HBM] * 5,
+        out_specs=(VMEM,) * 5,
+        scratch_shapes=[
+            pltpu.SMEM(counts.shape, jnp.int32),
+            pltpu.VMEM(materials.shape, jnp.int32),
+            pltpu.SMEM(coefficients.shape, F32),
+            pltpu.SemaphoreType.DMA((5,)),
+        ],
+        compiler_params=PARAMS,
+        cost_estimate=COST,
+        name="deposit_first",
+    )(*(pltpu.with_memory_space_constraint(value, pltpu.HBM) for value in inputs))
+
+
+def deposit(counts, cells, dose):
+    return pl.pallas_call(
+        functools.partial(deposit_kernel, 0),
         out_shape=f32(8, 16, 512),
-        in_specs=[SMEM, SMEM, VMEM, VMEM],
+        in_specs=[VMEM] * 3,
         out_specs=VMEM,
         compiler_params=PARAMS,
-        cost_estimate=pl.CostEstimate(flops=1 << 30, bytes_accessed=1 << 19, transcendentals=0),
+        cost_estimate=COST,
         name="deposit",
-    )(info, counts, cells, dose)
-
-
-def gather_kernel(info_ref, coef_ref, parts_ref, materials_ref, target_ref, *outs):
-    mid_ref, first_ref, second_ref = outs
-    even = info_ref[1] == 0
+    )(counts, cells, dose)
+
+
+def gather_kernel(parts_ref, spread_ref, target_ref, mid_ref, first_ref, second_ref):
+    even = lax.axis_index("gx") % 2 == 0
     strip = parts_ref[0]
     for z in range(1, parts_ref.shape[0]):
         strip = strip + parts_ref[z]
-    materials = materials_ref[...]
-    spread = jnp.zeros(materials.shape, F32)
-    for index in range(coef_ref.shape[0]):
-        spread = jnp.where(materials == index, coef_ref[index], spread)
-    for i, value in enumerate((strip, spread, target_ref[...])):
+    for i, value in enumerate((strip, spread_ref[...], target_ref[...])):
         mid_ref[i] = value
         left, right = value[:, :LANES], value[:, -LANES:]
         first_ref[i] = jnp.where(even, right, left)
         second_ref[i] = jnp.where(even, left, right)
 
 
-def widen_kernel(info_ref, mid_ref, first_ref, second_ref, wide_ref, send_ref, later_ref):
-    even, even_y = info_ref[1] == 0, info_ref[2] == 0
+def widen_kernel(mid_ref, first_ref, second_ref, wide_ref, send_ref, later_ref):
+    even, even_y = lax.axis_index("gx") % 2 == 0, lax.axis_index("gy") % 2 == 0
     near = lax.broadcasted_iota(jnp.int32, (16, LANES), 1) < LANES // 2
     for i in range(3):
         first, second = first_ref[i], second_ref[i]
@@ -129,8 +178,8 @@
     )
 
 
-def blur_kernel(info_ref, wide_ref, first_ref, second_ref, exposure_ref, adjoint_ref):
-    even = info_ref[2] == 0
+def blur_kernel(wide_ref, first_ref, second_ref, exposure_ref, adjoint_ref):
+    even = lax.axis_index("gy") % 2 == 0
     first, second = first_ref[...], second_ref[...]
     above, below = jnp.where(even, second, first), jnp.where(even, first, second)
     width = wide_ref.shape[2]
@@ -163,7 +212,6 @@
         high = table.astype(BF16)
         low = (table - high.astype(F32)).astype(BF16)
         both = jnp.concatenate([high, low], axis=0)
-        count = counts_ref[o]
         for k in range(0, slots, SPAN):
             chunk, lane = split(cells_ref[pl.ds(o, 1), k : k + SPAN])
             (cols,) = hot(lane, 8, [jnp.bfloat16(1)])
@@ -175,40 +223,39 @@
             for g in range(8):
                 value = jnp.where(chosen == iota + 8 * g, across[8 * g : 8 * g + 8], value)
             value = jnp.sum(value, axis=0, keepdims=True)
-            slot = lax.broadcasted_iota(jnp.int32, (1, SPAN), 1) + k
-            store(z, o, k, jnp.where(slot < count, value, 0.0))
+            store(z, o, k, jnp.where(alive(counts_ref, o, k), value, 0.0))
         return carry
 
     lax.fori_loop(0, table_ref.shape[0], strip, 0, unroll=4)
 
 
-def pick_kernel(info_ref, counts_ref, cells_ref, table_ref, out_ref):
+def pick_kernel(counts_ref, cells_ref, table_ref, out_ref):
     def store(z, o, k, value):
         out_ref[pl.ds(z, 1), k : k + SPAN] = value
 
-    pick_strips(info_ref[0], counts_ref, cells_ref, table_ref, store)
-
-
-def last_kernel(info_ref, counts_ref, cells_ref, table_ref, own_ref, out_ref):
+    pick_strips(own_core(), counts_ref, cells_ref, table_ref, store)
+
+
+def last_kernel(counts_ref, cells_ref, table_ref, own_ref, out_ref):
     def store(z, o, k, value):
         out_ref[pl.ds(o, 1), k : k + SPAN] = value
 
-    pick_strips(1 - info_ref[0], counts_ref, cells_ref, table_ref, store)
+    pick_strips(1 - own_core(), counts_ref, cells_ref, table_ref, store)
     for z in range(own_ref.shape[0]):
-        out_ref[pl.ds(2 * z + info_ref[0], 1), :] = own_ref[z : z + 1, :]
-
-
-def pick(info, counts, cells, table, own=None):
+        out_ref[pl.ds(2 * z + own_core(), 1), :] = own_ref[z : z + 1, :]
+
+
+def pick(counts, cells, table, own=None):
     last = own is not None
     return pl.pallas_call(
         last_kernel if last else pick_kernel,
         out_shape=f32(cells.shape[0] if last else table.shape[0], cells.shape[1]),
-        in_specs=[SMEM, SMEM] + [VMEM] * (3 if last else 2),
+        in_specs=[VMEM] * (4 if last else 3),
         out_specs=VMEM,
         compiler_params=PARAMS,
         cost_estimate=COST,
         name="pick_last" if last else "pick",
-    )(info, counts, cells, table, *([own] if last else []))
+    )(counts, cells, table, *([own] if last else []))
 
 
 def swap(value, axes, bits):
@@ -225,46 +272,46 @@
 def local(shot_cells, shot_dose, shot_counts, materials, coefficients, target):
     cells, dose, counts = shot_cells[0, 0, 0], shot_dose[0, 0, 0], shot_counts[0, 0, 0]
     shots = lax.axis_size("shots")
-    info = jnp.stack(
-        [lax.axis_index("shots") % 2, lax.axis_index("gx") % 2, lax.axis_index("gy") % 2]
-    ).astype(jnp.int32)
     lines = [[2 * z + c for z in range(shots // 2)] for c in range(2)]
 
     def exchange(value):
         return lax.all_to_all(value, "shots", 0, 0, axis_index_groups=lines, tiled=True)
 
-    away = swap(deposit(1, info, counts, cells, dose), "shots", 1)
-    parts = exchange(deposit(0, info, counts, cells, dose) + away)
+    away, counts, cells, dose, spread = deposit_first(
+        counts, coefficients, cells, dose, materials
+    )
+    away = swap(away, "shots", 1)
+    parts = exchange(deposit(counts, cells, dose) + away)
 
     mid, first, second = pl.pallas_call(
         gather_kernel,
         out_shape=(f32(3, 16, 512), f32(3, 16, LANES), f32(3, 16, LANES)),
-        in_specs=[SMEM] * 2 + [VMEM] * 3,
+        in_specs=[VMEM] * 3,
         out_specs=(VMEM,) * 3,
         compiler_params=PARAMS,
         name="gather",
-    )(info, coefficients, parts, materials, target)
+    )(parts, spread, target)
     wide, first, second = pl.pallas_call(
         widen_kernel,
         out_shape=(f32(3, 16, 640), f32(16, 640), f32(16, 640)),
-        in_specs=[SMEM] + [VMEM] * 3,
+        in_specs=[VMEM] * 3,
         out_specs=(VMEM,) * 3,
         compiler_params=PARAMS,
         name="widen",
-    )(info, mid, swap(first, "gx", 1), swap_later(second, "gx"))
+    )(mid, swap(first, "gx", 1), swap_later(second, "gx"))
     rows = ("shots", "gy")
     exposure, adjoint = pl.pallas_call(
         blur_kernel,
         out_shape=(f32(16, 512), f32(shots // 2, 64, LANES)),
-        in_specs=[SMEM] + [VMEM] * 3,
+        in_specs=[VMEM] * 3,
         out_specs=(VMEM,) * 2,
         compiler_params=PARAMS,
         name="blur",
-    )(info, wide, swap(first, rows, 1), swap_later(second, rows))
+    )(wide, swap(first, rows, 1), swap_later(second, rows))
 
     table = exchange(adjoint)
     other = swap(table, "shots", 1)
-    shot_grad = pick(info, counts, cells, other, pick(info, counts, cells, table))
+    shot_grad = pick(counts, cells, other, pick(counts, cells, table))
     return (exposure, shot_grad[None, None, None])
 
 

time: 70.8 us -> 65 us (0.918)
  Pallas kernels: 15.7 us -> 13 us
  local copies, waits for them, and re-layouts: 2.58 us -> 0.01 us
    unnamed x14 -> x2, local copies, waits for them, and re-layouts: 2.58 us -> 0.01 us
    pallas_call x2, Pallas kernels: 6.88 us -> 5.79 us  [pick(): pl.pallas_call(last_kernel if last else pick_kernel, out_shape=f32(cells....]
  transfers between devices with their start and end apart: 6 -> 6, of which waited for: 2 -> 2; matrix products, arithmetic and copies ran while one was open for 0% -> 0% of each run, Pallas kernels for 9% -> 8%
where the time goes in v3:
time: 65 us; the launch traced here: 64.7 us
  blocking collectives  32.2 us (50%)
  starting transfers between devices  14.5 us (22%)
  Pallas kernels  13 us (20%)
  waiting for transfers between devices  4.3 us (7%)
  between operations  0.73 us (1%)
    all_to_all x2, blocking collectives, exchange(): lax.all_to_all(value, 'shots', 0, 0, axis_index_groups=lines, tiled=True)  32.2 us
    ppermute x2, starting transfers between devices, swap_later(): return lax.ppermute(value, axes, pairs + [(j, i) for i, j in pairs])  7.77 us
    ppermute x4, starting transfers between devices, swap(): return lax.ppermute(value, axes, [(i, i ^ bits) for i in range(count)])  6.7 us
    pallas_call x2, Pallas kernels, pick(): pl.pallas_call(last_kernel if last else pick_kernel, out_shape=f32(cells....  5.79 us
    ppermute x2, waiting for transfers between devices, swap_later(): return lax.ppermute(value, axes, pairs + [(j, i) for i, j in pairs])  4.29 us
    pallas_call x1, Pallas kernels, deposit_first(): pl.pallas_call(first_kernel, out_shape=(f32(8, 16, 512), jax.ShapeDtypeSt...  3.61 us
    pallas_call x1, Pallas kernels, deposit(): pl.pallas_call(functools.partial(deposit_kernel, 0), out_shape=f32(8, 16,...  2.51 us
  transfers between devices with their start and end apart: 6, of which 2 were waited for; matrix products, arithmetic and copies ran while one was open for 0% of the time, Pallas kernels for 8%

profile of v3, /device:TPU:5, one launch (start us, length us, event | category | flops | bytes accessed | tf_op | source)
XLA Modules:
  0.0 64.7 jit_solution(10318381040189345978)
XLA Ops:
  0.6 3.6 %deposit_first.1 = (f32[8,16,512]{2,1,0:T(8,128)S(1)}, s32[16,128]{1,0:T(8,128)S(1)}, s32[16,4096]{1,0:T(8,128)S(1)}, f32[16,4096]{1,0:T(8,128)S(1)}, f32[16,512]{1,0:T(8,128)S(1)}) custom-call(s32[16]{0:T(128)} %bitcast.6, f32[4]{0:T(128)} %refs_1_.1, s32[16,4096]{1,0:T(8,128)} %bitcast.4, f32[16,4096]{1,0:T(8,128)} %bitcast.5, s32[16,512]{1,0:T(8,128)} %refs_4_.1), custom_call_target="tpu_custom_call" | custom-call | flops 1073741824 | bytes 262144 | tf_op jit(solution)/shard_map/deposit_first/pallas_call | solution.py:105
  4.3 0.8 %collective-permute-start = (f32[8,16,512]{2,1,0:T(8,128)S(1)}, f32[8,16,512]{2,1,0:T(8,128)S(1)}, u32[]{:S(2)}, u32[]{:S(2)}) collective-permute-start(f32[8,16,512]{2,1,0:T(8,128)S(1)} %get-tuple-element.18), channel_id=1, source_target_pairs={{0,16},{16,0},{32,48},{48,32},{64,80},{80,64},{96,112},{112,96},{1... | collective-permute-start | bytes 786440 | tf_op jit(solution)/shard_map/ppermute | solution.py:263
  5.0 2.5 %deposit.1 = f32[8,16,512]{2,1,0:T(8,128)S(1)} custom-call(s32[16,128]{1,0:T(8,128)S(1)} %get-tuple-element.15.counts_ref, s32[16,4096]{1,0:T(8,128)S(1)} %get-tuple-element.16.cells_ref, f32[16,4096]{1,0:T(8,128)S(1)} %get-tuple-element.17.dose_ref), custom_call_target="tpu_custom_call" | custom-call | flops 1073741824 | bytes 262144 | tf_op jit(solution)/shard_map/deposit/pallas_call | solution.py:129
  7.5 0.0 collective-permute-done
  7.6 0.0 copy-start
  7.6 20.4 %all_to_all.10.parts_ref = f32[8,16,512]{2,1,0:T(8,128)S(1)} all-to-all(f32[8,16,512]{2,1,0:T(8,128)S(1)} %add.3), channel_id=1, replica_groups={{0,32,64,96,128,160,192,224},{16,48,80,112,144,176,208,240},{1,33,65,97..., dimensions={0} | all-to-all | bytes 524288 | tf_op jit(solution)/shard_map/all_to_all | solution.py:278
  27.9 0.0 copy-done
  28.0 1.0 %collective-permute-start.1 = (f32[3,16,128]{2,1,0:T(8,128)S(1)}, f32[3,16,128]{2,1,0:T(8,128)S(1)}, u32[]{:S(2)}, u32[]{:S(2)}) collective-permute-start(f32[3,16,128]{2,1,0:T(8,128)S(1)} %get-tuple-element.21), channel_id=1, source_target_pairs={{0,1},{1,0},{2,3},{3,2},{4,5},{5,4},{6,7},{7,6},{8,9},{9,8},{10,11... | collective-permute-start | bytes 73736 | tf_op jit(solution)/shard_map/ppermute | solution.py:263
  29.0 1.9 %collective-permute-start.2 = (f32[3,16,128]{2,1,0:T(8,128)S(1)}, f32[3,16,128]{2,1,0:T(8,128)S(1)}, u32[]{:S(2)}, u32[]{:S(2)}) collective-permute-start(f32[3,16,128]{2,1,0:T(8,128)S(1)} %get-tuple-element.22), channel_id=1, source_target_pairs={{1,2},{2,1},{5,6},{6,5},{9,10},{10,9},{13,14},{14,13},{17,18},{18,... | collective-permute-start | bytes 73736 | tf_op jit(solution)/shard_map/ppermute | solution.py:269
  30.9 0.0 collective-permute-done.1.first_ref
  30.9 2.6 %collective-permute-done.2.second_ref = f32[3,16,128]{2,1,0:T(8,128)S(1)} collective-permute-done((f32[3,16,128]{2,1,0:T(8,128)S(1)}, f32[3,16,128]{2,1,0:T(8,128)S(1)}, u32[]{:S(2)}, u32[]{:S(2)}) %collective-permute-start.2) | collective-permute-done | bytes 24608 | tf_op jit(solution)/shard_map/ppermute | solution.py:269
  33.6 1.4 %collective-permute-start.3 = (f32[16,640]{1,0:T(8,128)S(1)}, f32[16,640]{1,0:T(8,128)S(1)}, u32[]{:S(2)}, u32[]{:S(2)}) collective-permute-start(f32[16,640]{1,0:T(8,128)S(1)} %get-tuple-element.24), channel_id=1, source_target_pairs={{0,4},{4,0},{8,12},{12,8},{16,20},{20,16},{24,28},{28,24},{32,36},... | collective-permute-start | bytes 122888 | tf_op jit(solution)/shard_map/ppermute | solution.py:263
  35.0 5.9 %collective-permute-start.4 = (f32[16,640]{1,0:T(8,128)S(1)}, f32[16,640]{1,0:T(8,128)S(1)}, u32[]{:S(2)}, u32[]{:S(2)}) collective-permute-start(f32[16,640]{1,0:T(8,128)S(1)} %get-tuple-element.25), channel_id=1, source_target_pairs={{4,8},{12,16},{20,24},{28,32},{36,40},{44,48},{52,56},{60,64},{68,... | collective-permute-start | bytes 122888 | tf_op jit(solution)/shard_map/ppermute | solution.py:269
  40.8 0.0 collective-permute-done.3.first_ref
  40.8 1.7 %collective-permute-done.4.second_ref = f32[16,640]{1,0:T(8,128)S(1)} collective-permute-done((f32[16,640]{1,0:T(8,128)S(1)}, f32[16,640]{1,0:T(8,128)S(1)}, u32[]{:S(2)}, u32[]{:S(2)}) %collective-permute-start.4) | collective-permute-done | bytes 40992 | tf_op jit(solution)/shard_map/ppermute | solution.py:269
  42.5 1.1 %blur.1 = (f32[16,512]{1,0:T(8,128)}, f32[8,64,128]{2,1,0:T(8,128)S(1)}) custom-call(f32[3,16,640]{2,1,0:T(8,128)S(1)} %get-tuple-element.23.wide_ref, f32[16,640]{1,0:T(8,128)S(1)} %collective-permute-done.3.first_ref, f32[16,640]{1,0:T(8,128)S(1)} %collective-permute-done.4.second_ref), custom_call_target="tpu_custom_call" | custom-call | tf_op jit(solution)/shard_map/blur/pallas_call | solution.py:303
  43.6 11.8 %all_to_all.11.table_ref = f32[8,64,128]{2,1,0:T(8,128)S(1)} all-to-all(f32[8,64,128]{2,1,0:T(8,128)S(1)} %get-tuple-element.27), channel_id=1, replica_groups={{0,32,64,96,128,160,192,224},{16,48,80,112,144,176,208,240},{1,33,65,97..., dimensions={0} | all-to-all | bytes 524288 | tf_op jit(solution)/shard_map/all_to_all | solution.py:278
  55.4 3.5 %collective-permute-start.5 = (f32[8,64,128]{2,1,0:T(8,128)S(1)}, f32[8,64,128]{2,1,0:T(8,128)S(1)}, u32[]{:S(2)}, u32[]{:S(2)}) collective-permute-start(f32[8,64,128]{2,1,0:T(8,128)S(1)} %all_to_all.11.table_ref), channel_id=1, source_target_pairs={{0,16},{16,0},{32,48},{48,32},{64,80},{80,64},{96,112},{112,96},{1... | collective-permute-start | bytes 786440 | tf_op jit(solution)/shard_map/ppermute | solution.py:263
  58.9 2.5 %pick.1.own_ref = f32[8,4096]{1,0:T(8,128)S(1)} custom-call(s32[16,128]{1,0:T(8,128)S(1)} %get-tuple-element.15.counts_ref, s32[16,4096]{1,0:T(8,128)S(1)} %get-tuple-element.16.cells_ref, f32[8,64,128]{2,1,0:T(8,128)S(1)} %all_to_all.11.table_ref), custom_call_target="tpu_custom_call" | custom-call | flops 1073741824 | bytes 262144 | tf_op jit(solution)/shard_map/pick/pallas_call | solution.py:250
  61.5 0.0 collective-permute-done.5.table_ref
  61.5 3.3 %pick_last.1 = f32[16,4096]{1,0:T(8,128)} custom-call(s32[16,128]{1,0:T(8,128)S(1)} %get-tuple-element.15.counts_ref, s32[16,4096]{1,0:T(8,128)S(1)} %get-tuple-element.16.cells_ref, f32[8,64,128]{2,1,0:T(8,128)S(1)} %collective-permute-done.5.table_ref, f32[8,4096]{1,0:T(8,128)S(1)} %pick.1.own_ref), custom_call_target="tpu_custom_call" | custom-call | flops 1073741824 | bytes 262144 | tf_op jit(solution)/shard_map/pick_last/pallas_call | solution.py:250
  (3 shorter events, 0.1 us)
Async XLA Ops:
  4.3 3.3 %collective-permute-start = (f32[8,16,512]{2,1,0:T(8,128)S(1)}, f32[8,16,512]{2,1,0:T(8,128)S(1)}, u32[]{:S(2)}, u32[]{:S(2)}) collective-permute-start(f32[8,16,512]{2,1,0:T(8,128)S(1)} %get-tuple-element.18), channel_id=1, source_target_pairs={{0,16},{16,0},{32,48},{48,32},{64,80},{80,64},{96,112},{112,96},{1... | collective-permute-start | bytes 786440 | tf_op jit(solution)/shard_map/ppermute | solution.py:263
  7.6 20.4 %copy-start = (f32[16,512]{1,0:T(8,128)S(1)}, f32[16,512]{1,0:T(8,128)}, u32[]{:S(2)}) copy-start(f32[16,512]{1,0:T(8,128)} %target_ref.1) | copy-start | bytes 98308
  28.0 2.9 %collective-permute-start.1 = (f32[3,16,128]{2,1,0:T(8,128)S(1)}, f32[3,16,128]{2,1,0:T(8,128)S(1)}, u32[]{:S(2)}, u32[]{:S(2)}) collective-permute-start(f32[3,16,128]{2,1,0:T(8,128)S(1)} %get-tuple-element.21), channel_id=1, source_target_pairs={{0,1},{1,0},{2,3},{3,2},{4,5},{5,4},{6,7},{7,6},{8,9},{9,8},{10,11... | collective-permute-start | bytes 73736 | tf_op jit(solution)/shard_map/ppermute | solution.py:263
  29.0 4.6 %collective-permute-start.2 = (f32[3,16,128]{2,1,0:T(8,128)S(1)}, f32[3,16,128]{2,1,0:T(8,128)S(1)}, u32[]{:S(2)}, u32[]{:S(2)}) collective-permute-start(f32[3,16,128]{2,1,0:T(8,128)S(1)} %get-tuple-element.22), channel_id=1, source_target_pairs={{1,2},{2,1},{5,6},{6,5},{9,10},{10,9},{13,14},{14,13},{17,18},{18,... | collective-permute-start | bytes 73736 | tf_op jit(solution)/shard_map/ppermute | solution.py:269
  33.6 7.3 %collective-permute-start.3 = (f32[16,640]{1,0:T(8,128)S(1)}, f32[16,640]{1,0:T(8,128)S(1)}, u32[]{:S(2)}, u32[]{:S(2)}) collective-permute-start(f32[16,640]{1,0:T(8,128)S(1)} %get-tuple-element.24), channel_id=1, source_target_pairs={{0,4},{4,0},{8,12},{12,8},{16,20},{20,16},{24,28},{28,24},{32,36},... | collective-permute-start | bytes 122888 | tf_op jit(solution)/shard_map/ppermute | solution.py:263
  35.0 7.5 %collective-permute-start.4 = (f32[16,640]{1,0:T(8,128)S(1)}, f32[16,640]{1,0:T(8,128)S(1)}, u32[]{:S(2)}, u32[]{:S(2)}) collective-permute-start(f32[16,640]{1,0:T(8,128)S(1)} %get-tuple-element.25), channel_id=1, source_target_pairs={{4,8},{12,16},{20,24},{28,32},{36,40},{44,48},{52,56},{60,64},{68,... | collective-permute-start | bytes 122888 | tf_op jit(solution)/shard_map/ppermute | solution.py:269
  55.4 6.1 %collective-permute-start.5 = (f32[8,64,128]{2,1,0:T(8,128)S(1)}, f32[8,64,128]{2,1,0:T(8,128)S(1)}, u32[]{:S(2)}, u32[]{:S(2)}) collective-permute-start(f32[8,64,128]{2,1,0:T(8,128)S(1)} %all_to_all.11.table_ref), channel_id=1, source_target_pairs={{0,16},{16,0},{32,48},{48,32},{64,80},{80,64},{96,112},{112,96},{1... | collective-permute-start | bytes 786440 | tf_op jit(solution)/shard_map/ppermute | solution.py:263

commit v4 on v3

--- a/solution.py
+++ b/solution.py
@@ -9,6 +9,8 @@
 
 STEPS = 3
 SPAN = 512
+CHUNK = 1024
+UNROLL = 8
 LANES = 128
 VMEM = pl.BlockSpec(memory_space=pltpu.VMEM)
 HBM = pl.BlockSpec(memory_space=pltpu.HBM)
@@ -75,7 +77,7 @@
             out_ref[j, :, q * LANES : (q + 1) * LANES] = both[16 * q : 16 * q + 16]
         return carry
 
-    lax.fori_loop(0, out_ref.shape[0], strip, 0, unroll=4)
+    lax.fori_loop(0, out_ref.shape[0], strip, 0, unroll=UNROLL)
 
 
 def first_kernel(*refs):
@@ -142,21 +144,29 @@
     strip = parts_ref[0]
     for z in range(1, parts_ref.shape[0]):
         strip = strip + parts_ref[z]
+    lane = lax.broadcasted_iota(jnp.int32, (16, LANES), 1)
+    left, right = jnp.zeros((16, LANES), F32), jnp.zeros((16, LANES), F32)
     for i, value in enumerate((strip, spread_ref[...], target_ref[...])):
         mid_ref[i] = value
-        left, right = value[:, :LANES], value[:, -LANES:]
-        first_ref[i] = jnp.where(even, right, left)
-        second_ref[i] = jnp.where(even, left, right)
+        here = (lane >= 16 * i) & (lane < 16 * i + 8)
+        left = jnp.where(here, pltpu.roll(value[:, :LANES], 16 * i, 1), left)
+        right = jnp.where(here, pltpu.roll(value[:, -LANES:], 16 * i + 8, 1), right)
+    first_ref[...] = jnp.where(even, right, left)
+    second_ref[...] = jnp.where(even, left, right)
 
 
 def widen_kernel(mid_ref, first_ref, second_ref, wide_ref, send_ref, later_ref):
     even, even_y = lax.axis_index("gx") % 2 == 0, lax.axis_index("gy") % 2 == 0
     near = lax.broadcasted_iota(jnp.int32, (16, LANES), 1) < LANES // 2
+    first, second = first_ref[...], second_ref[...]
+    left, right = jnp.where(even, second, first), jnp.where(even, first, second)
     for i in range(3):
-        first, second = first_ref[i], second_ref[i]
-        left = jnp.where(even, second, first)
-        right = jnp.where(even, first, second)
-        wide = jnp.concatenate([mid_ref[i], jnp.where(near, right, left)], axis=1)
+        tile = jnp.where(
+            near,
+            pltpu.roll(right, (LANES - 16 * i) % LANES, 1),
+            pltpu.roll(left, LANES - 8 - 16 * i, 1),
+        )
+        wide = jnp.concatenate([mid_ref[i], tile], axis=1)
         wide_ref[i] = wide
         if i == 0:
             top, bottom = wide[:8], wide[8:]
@@ -203,59 +213,95 @@
             adjoint_ref[z, 16 * q : 16 * q + 16] = field[8:24, q * LANES : (q + 1) * LANES]
 
 
-def pick_strips(core, counts_ref, cells_ref, table_ref, store):
-    slots = cells_ref.shape[1]
+def parts_of(table):
+    high = table.astype(BF16)
+    return jnp.concatenate([high, (table - high.astype(F32)).astype(BF16)], axis=0)
+
+
+def pick_span(counts_ref, cells_ref, both, o, k):
+    span = pl.ds(k, SPAN)
+    chunk, lane = split(cells_ref[pl.ds(o, 1), span])
+    (cols,) = hot(lane, 8, [jnp.bfloat16(1)])
+    across = jnp.dot(both, cols, preferred_element_type=F32)
+    across = across[:64] + across[64:]
+    iota = lax.broadcasted_iota(jnp.int32, (8, SPAN), 0)
+    chosen = jnp.broadcast_to(chunk, (8, SPAN))
+    value = jnp.zeros((8, SPAN), F32)
+    for g in range(8):
+        value = jnp.where(chosen == iota + 8 * g, across[8 * g : 8 * g + 8], value)
+    value = jnp.sum(value, axis=0, keepdims=True)
+    return jnp.where(alive(counts_ref, o, k), value, 0.0)
+
+
+def pick_kernel(counts_ref, cells_ref, table_ref, blurred_ref, own_ref, exposure_hbm, sem):
+    copy = pltpu.make_async_copy(blurred_ref, exposure_hbm, sem)
+    copy.start()
 
     def strip(z, carry):
-        o = 2 * z + core
-        table = table_ref[z]
-        high = table.astype(BF16)
-        low = (table - high.astype(F32)).astype(BF16)
-        both = jnp.concatenate([high, low], axis=0)
-        for k in range(0, slots, SPAN):
-            chunk, lane = split(cells_ref[pl.ds(o, 1), k : k + SPAN])
-            (cols,) = hot(lane, 8, [jnp.bfloat16(1)])
-            across = jnp.dot(both, cols, preferred_element_type=F32)
-            across = across[:64] + across[64:]
-            iota = lax.broadcasted_iota(jnp.int32, (8, SPAN), 0)
-            chosen = jnp.broadcast_to(chunk, (8, SPAN))
-            value = jnp.zeros((8, SPAN), F32)
-            for g in range(8):
-                value = jnp.where(chosen == iota + 8 * g, across[8 * g : 8 * g + 8], value)
-            value = jnp.sum(value, axis=0, keepdims=True)
-            store(z, o, k, jnp.where(alive(counts_ref, o, k), value, 0.0))
+        both = parts_of(table_ref[z])
+        for k in range(0, cells_ref.shape[1], SPAN):
+            value = pick_span(counts_ref, cells_ref, both, 2 * z + own_core(), k)
+            own_ref[pl.ds(z, 1), k : k + SPAN] = value
         return carry
 
-    lax.fori_loop(0, table_ref.shape[0], strip, 0, unroll=4)
-
-
-def pick_kernel(counts_ref, cells_ref, table_ref, out_ref):
-    def store(z, o, k, value):
-        out_ref[pl.ds(z, 1), k : k + SPAN] = value
-
-    pick_strips(own_core(), counts_ref, cells_ref, table_ref, store)
-
-
-def last_kernel(counts_ref, cells_ref, table_ref, own_ref, out_ref):
-    def store(z, o, k, value):
-        out_ref[pl.ds(o, 1), k : k + SPAN] = value
-
-    pick_strips(1 - own_core(), counts_ref, cells_ref, table_ref, store)
-    for z in range(own_ref.shape[0]):
-        out_ref[pl.ds(2 * z + own_core(), 1), :] = own_ref[z : z + 1, :]
-
-
-def pick(counts, cells, table, own=None):
-    last = own is not None
+    lax.fori_loop(0, table_ref.shape[0], strip, 0, unroll=UNROLL)
+    copy.wait()
+
+
+def pick(counts, cells, table, blurred):
     return pl.pallas_call(
-        last_kernel if last else pick_kernel,
-        out_shape=f32(cells.shape[0] if last else table.shape[0], cells.shape[1]),
-        in_specs=[VMEM] * (4 if last else 3),
-        out_specs=VMEM,
+        pick_kernel,
+        out_shape=(f32(table.shape[0], cells.shape[1]), f32(*blurred.shape)),
+        in_specs=[VMEM] * 4,
+        out_specs=(VMEM, pl.BlockSpec(memory_space=pl.ANY)),
+        scratch_shapes=[pltpu.SemaphoreType.DMA],
         compiler_params=PARAMS,
         cost_estimate=COST,
-        name="pick_last" if last else "pick",
-    )(counts, cells, table, *([own] if last else []))
+        name="pick",
+    )(counts, cells, table, blurred)
+
+
+def last_kernel(counts_ref, cells_ref, table_ref, own_ref, out_hbm, out_ref, both_ref, sems):
+    depth, core = table_ref.shape[0], own_core()
+    for z in range(depth):
+        out_ref[pl.ds(2 * z + core, 1), :] = own_ref[z : z + 1, :]
+        both_ref[z] = parts_of(table_ref[z])
+
+    def copy(i):
+        part = pl.ds(pl.multiple_of(i * CHUNK, CHUNK), CHUNK)
+        return pltpu.make_async_copy(out_ref.at[:, part], out_hbm.at[:, part], sems.at[i])
+
+    def chunk(i, carry):
+        for z in range(depth):
+            o = 2 * z + 1 - core
+            for j in range(0, CHUNK, SPAN):
+                k = pl.multiple_of(i * CHUNK + j, SPAN)
+                value = pick_span(counts_ref, cells_ref, both_ref[z], o, k)
+                out_ref[pl.ds(o, 1), pl.ds(k, SPAN)] = value
+        copy(i).start()
+        return carry
+
+    steps = cells_ref.shape[1] // CHUNK
+    lax.fori_loop(0, steps, chunk, 0, unroll=True)
+    for i in range(steps):
+        copy(i).wait()
+
+
+def pick_last(counts, cells, table, own):
+    return pl.pallas_call(
+        last_kernel,
+        out_shape=f32(*cells.shape),
+        in_specs=[VMEM] * 4,
+        out_specs=pl.BlockSpec(memory_space=pl.ANY),
+        scratch_shapes=[
+            pltpu.VMEM(cells.shape, F32),
+            pltpu.VMEM((table.shape[0], 2 * 64, LANES), BF16),
+            pltpu.SemaphoreType.DMA((cells.shape[1] // CHUNK,)),
+        ],
+        compiler_params=PARAMS,
+        cost_estimate=COST,
+        name="pick_last",
+    )(counts, cells, table, own)
 
 
 def swap(value, axes, bits):
@@ -285,7 +331,7 @@
 
     mid, first, second = pl.pallas_call(
         gather_kernel,
-        out_shape=(f32(3, 16, 512), f32(3, 16, LANES), f32(3, 16, LANES)),
+        out_shape=(f32(3, 16, 512), f32(16, LANES), f32(16, LANES)),
         in_specs=[VMEM] * 3,
         out_specs=(VMEM,) * 3,
         compiler_params=PARAMS,
@@ -300,7 +346,7 @@
         name="widen",
     )(mid, swap(first, "gx", 1), swap_later(second, "gx"))
     rows = ("shots", "gy")
-    exposure, adjoint = pl.pallas_call(
+    blurred, adjoint = pl.pallas_call(
         blur_kernel,
         out_shape=(f32(16, 512), f32(shots // 2, 64, LANES)),
         in_specs=[VMEM] * 3,
@@ -311,7 +357,8 @@
 
     table = exchange(adjoint)
     other = swap(table, "shots", 1)
-    shot_grad = pick(counts, cells, other, pick(counts, cells, table))
+    own, exposure = pick(counts, cells, table, blurred)
+    shot_grad = pick_last(counts, cells, other, own)
     return (exposure, shot_grad[None, None, None])
 
 

time: 65 us -> 63.7 us (0.980)
  Pallas kernels: 13 us -> 11.9 us
  transfers between devices with their start and end apart: 6 -> 6, of which waited for: 2 -> 2; matrix products, arithmetic and copies ran while one was open for 0% -> 0% of each run, Pallas kernels for 8% -> 7%
where the time goes in v4:
time: 63.7 us; the launch traced here: 63.4 us
  blocking collectives  32.2 us (51%)
  starting transfers between devices  14.4 us (23%)
  Pallas kernels  11.9 us (19%)
  waiting for transfers between devices  4.13 us (6%)
  between operations  0.73 us (1%)
    all_to_all x2, blocking collectives, exchange(): lax.all_to_all(value, 'shots', 0, 0, axis_index_groups=lines, tiled=True)  32.2 us
    ppermute x2, starting transfers between devices, swap_later(): return lax.ppermute(value, axes, pairs + [(j, i) for i, j in pairs])  7.76 us
    ppermute x4, starting transfers between devices, swap(): return lax.ppermute(value, axes, [(i, i ^ bits) for i in range(count)])  6.67 us
    ppermute x2, waiting for transfers between devices, swap_later(): return lax.ppermute(value, axes, pairs + [(j, i) for i, j in pairs])  4.12 us
    pallas_call x1, Pallas kernels, deposit_first(): pl.pallas_call(first_kernel, out_shape=(f32(8, 16, 512), jax.ShapeDtypeSt...  3.43 us
    pallas_call x1, Pallas kernels, pick_last(): pl.pallas_call(last_kernel, out_shape=f32(*cells.shape), in_specs=[VMEM]...  3.07 us
    pallas_call x1, Pallas kernels, pick(): pl.pallas_call(pick_kernel, out_shape=(f32(table.shape[0], cells.shape[1]...  2.37 us
    pallas_call x1, Pallas kernels, deposit(): pl.pallas_call(functools.partial(deposit_kernel, 0), out_shape=f32(8, 16,...  2.34 us
  transfers between devices with their start and end apart: 6, of which 2 were waited for; matrix products, arithmetic and copies ran while one was open for 0% of the time, Pallas kernels for 7%

profile of v4, /device:TPU:5, one launch (start us, length us, event | category | flops | bytes accessed | tf_op | source)
XLA Modules:
  0.0 63.4 jit_solution(871724048020498376)
XLA Ops:
  0.6 3.4 %deposit_first.1 = (f32[8,16,512]{2,1,0:T(8,128)S(1)}, s32[16,128]{1,0:T(8,128)S(1)}, s32[16,4096]{1,0:T(8,128)S(1)}, f32[16,4096]{1,0:T(8,128)S(1)}, f32[16,512]{1,0:T(8,128)S(1)}) custom-call(s32[16]{0:T(128)} %bitcast.6, f32[4]{0:T(128)} %refs_1_.1, s32[16,4096]{1,0:T(8,128)} %bitcast.4, f32[16,4096]{1,0:T(8,128)} %bitcast.5, s32[16,512]{1,0:T(8,128)} %refs_4_.1), custom_call_target="tpu_custom_call" | custom-call | flops 1073741824 | bytes 262144 | tf_op jit(solution)/shard_map/deposit_first/pallas_call | solution.py:107
  4.1 0.8 %collective-permute-start = (f32[8,16,512]{2,1,0:T(8,128)S(1)}, f32[8,16,512]{2,1,0:T(8,128)S(1)}, u32[]{:S(2)}, u32[]{:S(2)}) collective-permute-start(f32[8,16,512]{2,1,0:T(8,128)S(1)} %get-tuple-element.20), channel_id=1, source_target_pairs={{0,16},{16,0},{32,48},{48,32},{64,80},{80,64},{96,112},{112,96},{1... | collective-permute-start | bytes 786440 | tf_op jit(solution)/shard_map/ppermute | solution.py:309
  4.8 2.3 %deposit.1 = f32[8,16,512]{2,1,0:T(8,128)S(1)} custom-call(s32[16,128]{1,0:T(8,128)S(1)} %get-tuple-element.17.counts_ref, s32[16,4096]{1,0:T(8,128)S(1)} %get-tuple-element.18.cells_ref, f32[16,4096]{1,0:T(8,128)S(1)} %get-tuple-element.19.dose_ref), custom_call_target="tpu_custom_call" | custom-call | flops 1073741824 | bytes 262144 | tf_op jit(solution)/shard_map/deposit/pallas_call | solution.py:131
  7.2 0.0 collective-permute-done
  7.2 0.0 copy-start
  7.2 20.3 %all_to_all.10.parts_ref = f32[8,16,512]{2,1,0:T(8,128)S(1)} all-to-all(f32[8,16,512]{2,1,0:T(8,128)S(1)} %add.3), channel_id=1, replica_groups={{0,32,64,96,128,160,192,224},{16,48,80,112,144,176,208,240},{1,33,65,97..., dimensions={0} | all-to-all | bytes 524288 | tf_op jit(solution)/shard_map/all_to_all | solution.py:324
  27.6 0.0 copy-done
  27.6 0.1 gather.1
  27.7 1.0 %collective-permute-start.1 = (f32[16,128]{1,0:T(8,128)S(1)}, f32[16,128]{1,0:T(8,128)S(1)}, u32[]{:S(2)}, u32[]{:S(2)}) collective-permute-start(f32[16,128]{1,0:T(8,128)S(1)} %get-tuple-element.23), channel_id=1, source_target_pairs={{0,1},{1,0},{2,3},{3,2},{4,5},{5,4},{6,7},{7,6},{8,9},{9,8},{10,11... | collective-permute-start | bytes 24584 | tf_op jit(solution)/shard_map/ppermute | solution.py:309
  28.7 1.9 %collective-permute-start.2 = (f32[16,128]{1,0:T(8,128)S(1)}, f32[16,128]{1,0:T(8,128)S(1)}, u32[]{:S(2)}, u32[]{:S(2)}) collective-permute-start(f32[16,128]{1,0:T(8,128)S(1)} %get-tuple-element.24), channel_id=1, source_target_pairs={{1,2},{2,1},{5,6},{6,5},{9,10},{10,9},{13,14},{14,13},{17,18},{18,... | collective-permute-start | bytes 24584 | tf_op jit(solution)/shard_map/ppermute | solution.py:315
  30.6 0.0 collective-permute-done.1.first_ref
  30.6 2.5 %collective-permute-done.2.second_ref = f32[16,128]{1,0:T(8,128)S(1)} collective-permute-done((f32[16,128]{1,0:T(8,128)S(1)}, f32[16,128]{1,0:T(8,128)S(1)}, u32[]{:S(2)}, u32[]{:S(2)}) %collective-permute-start.2) | collective-permute-done | bytes 8224 | tf_op jit(solution)/shard_map/ppermute | solution.py:315
  33.1 0.1 widen.1
  33.2 1.3 %collective-permute-start.3 = (f32[16,640]{1,0:T(8,128)S(1)}, f32[16,640]{1,0:T(8,128)S(1)}, u32[]{:S(2)}, u32[]{:S(2)}) collective-permute-start(f32[16,640]{1,0:T(8,128)S(1)} %get-tuple-element.26), channel_id=1, source_target_pairs={{0,4},{4,0},{8,12},{12,8},{16,20},{20,16},{24,28},{28,24},{32,36},... | collective-permute-start | bytes 122888 | tf_op jit(solution)/shard_map/ppermute | solution.py:309
  34.5 5.8 %collective-permute-start.4 = (f32[16,640]{1,0:T(8,128)S(1)}, f32[16,640]{1,0:T(8,128)S(1)}, u32[]{:S(2)}, u32[]{:S(2)}) collective-permute-start(f32[16,640]{1,0:T(8,128)S(1)} %get-tuple-element.27), channel_id=1, source_target_pairs={{4,8},{12,16},{20,24},{28,32},{36,40},{44,48},{52,56},{60,64},{68,... | collective-permute-start | bytes 122888 | tf_op jit(solution)/shard_map/ppermute | solution.py:315
  40.4 0.0 collective-permute-done.3.first_ref
  40.4 1.7 %collective-permute-done.4.second_ref = f32[16,640]{1,0:T(8,128)S(1)} collective-permute-done((f32[16,640]{1,0:T(8,128)S(1)}, f32[16,640]{1,0:T(8,128)S(1)}, u32[]{:S(2)}, u32[]{:S(2)}) %collective-permute-start.4) | collective-permute-done | bytes 40992 | tf_op jit(solution)/shard_map/ppermute | solution.py:315
  42.0 0.5 blur.1
  42.6 11.8 %all_to_all.11.table_ref = f32[8,64,128]{2,1,0:T(8,128)S(1)} all-to-all(f32[8,64,128]{2,1,0:T(8,128)S(1)} %get-tuple-element.28), channel_id=1, replica_groups={{0,32,64,96,128,160,192,224},{16,48,80,112,144,176,208,240},{1,33,65,97..., dimensions={0} | all-to-all | bytes 524288 | tf_op jit(solution)/shard_map/all_to_all | solution.py:324
  54.4 3.6 %collective-permute-start.5 = (f32[8,64,128]{2,1,0:T(8,128)S(1)}, f32[8,64,128]{2,1,0:T(8,128)S(1)}, u32[]{:S(2)}, u32[]{:S(2)}) collective-permute-start(f32[8,64,128]{2,1,0:T(8,128)S(1)} %all_to_all.11.table_ref), channel_id=1, source_target_pairs={{0,16},{16,0},{32,48},{48,32},{64,80},{80,64},{96,112},{112,96},{1... | collective-permute-start | bytes 786440 | tf_op jit(solution)/shard_map/ppermute | solution.py:309
  58.0 2.4 %pick.1 = (f32[8,4096]{1,0:T(8,128)S(1)}, f32[16,512]{1,0:T(8,128)}) custom-call(s32[16,128]{1,0:T(8,128)S(1)} %get-tuple-element.17.counts_ref, s32[16,4096]{1,0:T(8,128)S(1)} %get-tuple-element.18.cells_ref, f32[8,64,128]{2,1,0:T(8,128)S(1)} %all_to_all.11.table_ref, f32[16,512]{1,0:T(8,128)S(1)} %get-tuple-element.29.blurred_ref), custom_call_target="tpu_custom_call" | custom-call | flops 1073741824 | bytes 262144 | tf_op jit(solution)/shard_map/pick/pallas_call | solution.py:252
  60.4 0.0 collective-permute-done.5.table_ref
  60.4 3.1 %pick_last.1 = f32[16,4096]{1,0:T(8,128)} custom-call(s32[16,128]{1,0:T(8,128)S(1)} %get-tuple-element.17.counts_ref, s32[16,4096]{1,0:T(8,128)S(1)} %get-tuple-element.18.cells_ref, f32[8,64,128]{2,1,0:T(8,128)S(1)} %collective-permute-done.5.table_ref, f32[8,4096]{1,0:T(8,128)S(1)} %get-tuple-element.31.own_ref), custom_call_target="tpu_custom_call" | custom-call | flops 1073741824 | bytes 262144 | tf_op jit(solution)/shard_map/pick_last/pallas_call | solution.py:291
  (1 shorter events, 0.0 us)
Async XLA Ops:
  4.1 3.1 %collective-permute-start = (f32[8,16,512]{2,1,0:T(8,128)S(1)}, f32[8,16,512]{2,1,0:T(8,128)S(1)}, u32[]{:S(2)}, u32[]{:S(2)}) collective-permute-start(f32[8,16,512]{2,1,0:T(8,128)S(1)} %get-tuple-element.20), channel_id=1, source_target_pairs={{0,16},{16,0},{32,48},{48,32},{64,80},{80,64},{96,112},{112,96},{1... | collective-permute-start | bytes 786440 | tf_op jit(solution)/shard_map/ppermute | solution.py:309
  7.2 20.4 %copy-start = (f32[16,512]{1,0:T(8,128)S(1)}, f32[16,512]{1,0:T(8,128)}, u32[]{:S(2)}) copy-start(f32[16,512]{1,0:T(8,128)} %target_ref.1) | copy-start | bytes 98308
  27.7 2.9 %collective-permute-start.1 = (f32[16,128]{1,0:T(8,128)S(1)}, f32[16,128]{1,0:T(8,128)S(1)}, u32[]{:S(2)}, u32[]{:S(2)}) collective-permute-start(f32[16,128]{1,0:T(8,128)S(1)} %get-tuple-element.23), channel_id=1, source_target_pairs={{0,1},{1,0},{2,3},{3,2},{4,5},{5,4},{6,7},{7,6},{8,9},{9,8},{10,11... | collective-permute-start | bytes 24584 | tf_op jit(solution)/shard_map/ppermute | solution.py:309
  28.7 4.4 %collective-permute-start.2 = (f32[16,128]{1,0:T(8,128)S(1)}, f32[16,128]{1,0:T(8,128)S(1)}, u32[]{:S(2)}, u32[]{:S(2)}) collective-permute-start(f32[16,128]{1,0:T(8,128)S(1)} %get-tuple-element.24), channel_id=1, source_target_pairs={{1,2},{2,1},{5,6},{6,5},{9,10},{10,9},{13,14},{14,13},{17,18},{18,... | collective-permute-start | bytes 24584 | tf_op jit(solution)/shard_map/ppermute | solution.py:315
  33.2 7.2 %collective-permute-start.3 = (f32[16,640]{1,0:T(8,128)S(1)}, f32[16,640]{1,0:T(8,128)S(1)}, u32[]{:S(2)}, u32[]{:S(2)}) collective-permute-start(f32[16,640]{1,0:T(8,128)S(1)} %get-tuple-element.26), channel_id=1, source_target_pairs={{0,4},{4,0},{8,12},{12,8},{16,20},{20,16},{24,28},{28,24},{32,36},... | collective-permute-start | bytes 122888 | tf_op jit(solution)/shard_map/ppermute | solution.py:309
  34.5 7.5 %collective-permute-start.4 = (f32[16,640]{1,0:T(8,128)S(1)}, f32[16,640]{1,0:T(8,128)S(1)}, u32[]{:S(2)}, u32[]{:S(2)}) collective-permute-start(f32[16,640]{1,0:T(8,128)S(1)} %get-tuple-element.27), channel_id=1, source_target_pairs={{4,8},{12,16},{20,24},{28,32},{36,40},{44,48},{52,56},{60,64},{68,... | collective-permute-start | bytes 122888 | tf_op jit(solution)/shard_map/ppermute | solution.py:315
  54.4 5.9 %collective-permute-start.5 = (f32[8,64,128]{2,1,0:T(8,128)S(1)}, f32[8,64,128]{2,1,0:T(8,128)S(1)}, u32[]{:S(2)}, u32[]{:S(2)}) collective-permute-start(f32[8,64,128]{2,1,0:T(8,128)S(1)} %all_to_all.11.table_ref), channel_id=1, source_target_pairs={{0,16},{16,0},{32,48},{48,32},{64,80},{80,64},{96,112},{112,96},{1... | collective-permute-start | bytes 786440 | tf_op jit(solution)/shard_map/ppermute | solution.py:309

commit v5 on v4

--- a/solution.py
+++ b/solution.py
@@ -140,7 +140,6 @@
 
 
 def gather_kernel(parts_ref, spread_ref, target_ref, mid_ref, first_ref, second_ref):
-    even = lax.axis_index("gx") % 2 == 0
     strip = parts_ref[0]
     for z in range(1, parts_ref.shape[0]):
         strip = strip + parts_ref[z]
@@ -151,15 +150,14 @@
         here = (lane >= 16 * i) & (lane < 16 * i + 8)
         left = jnp.where(here, pltpu.roll(value[:, :LANES], 16 * i, 1), left)
         right = jnp.where(here, pltpu.roll(value[:, -LANES:], 16 * i + 8, 1), right)
-    first_ref[...] = jnp.where(even, right, left)
-    second_ref[...] = jnp.where(even, left, right)
+    column, columns = lax.axis_index("gx"), lax.axis_size("gx")
+    first_ref[...] = jnp.where(column == columns - 1, 0.0, right)
+    second_ref[...] = jnp.where(column == 0, 0.0, left)
 
 
 def widen_kernel(mid_ref, first_ref, second_ref, wide_ref, send_ref, later_ref):
-    even, even_y = lax.axis_index("gx") % 2 == 0, lax.axis_index("gy") % 2 == 0
     near = lax.broadcasted_iota(jnp.int32, (16, LANES), 1) < LANES // 2
-    first, second = first_ref[...], second_ref[...]
-    left, right = jnp.where(even, second, first), jnp.where(even, first, second)
+    left, right = first_ref[...], second_ref[...]
     for i in range(3):
         tile = jnp.where(
             near,
@@ -174,8 +172,10 @@
             top, bottom = jnp.concatenate([top, wide[:5]]), jnp.concatenate([bottom, wide[11:]])
         else:
             top, bottom = jnp.concatenate([top, wide[:3]]), jnp.concatenate([bottom, wide[13:]])
-    send_ref[...] = jnp.where(even_y, bottom, top)
-    later_ref[...] = jnp.where(even_y, top, bottom)
+    line = lax.axis_index("shots") * lax.axis_size("gy") + lax.axis_index("gy")
+    last = lax.axis_size("shots") * lax.axis_size("gy") - 1
+    send_ref[...] = jnp.where(line == last, 0.0, bottom)
+    later_ref[...] = jnp.where(line == 0, 0.0, top)
 
 
 def neighbours(field):
@@ -189,9 +189,7 @@
 
 
 def blur_kernel(wide_ref, first_ref, second_ref, exposure_ref, adjoint_ref):
-    even = lax.axis_index("gy") % 2 == 0
-    first, second = first_ref[...], second_ref[...]
-    above, below = jnp.where(even, second, first), jnp.where(even, first, second)
+    above, below = first_ref[...], second_ref[...]
     width = wide_ref.shape[2]
     blank = lambda rows: jnp.zeros((rows, width), F32)
     field = jnp.concatenate([above[:8], wide_ref[0], below[:8]], axis=0)
@@ -309,10 +307,9 @@
     return lax.ppermute(value, axes, [(i, i ^ bits) for i in range(count)])
 
 
-def swap_later(value, axes):
+def shift(value, axes, by):
     count = lax.axis_size(axes)
-    pairs = [(i, i + 1) for i in range(1, count - 1, 2)]
-    return lax.ppermute(value, axes, pairs + [(j, i) for i, j in pairs])
+    return lax.ppermute(value, axes, [(i, (i + by) % count) for i in range(count)])
 
 
 def local(shot_cells, shot_dose, shot_counts, materials, coefficients, target):
@@ -344,7 +341,7 @@
         out_specs=(VMEM,) * 3,
         compiler_params=PARAMS,
         name="widen",
-    )(mid, swap(first, "gx", 1), swap_later(second, "gx"))
+    )(mid, shift(first, "gx", 1), shift(second, "gx", -1))
     rows = ("shots", "gy")
     blurred, adjoint = pl.pallas_call(
         blur_kernel,
@@ -353,7 +350,7 @@
         out_specs=(VMEM,) * 2,
         compiler_params=PARAMS,
         name="blur",
-    )(wide, swap(first, rows, 1), swap_later(second, rows))
+    )(wide, shift(first, rows, 1), shift(second, rows, -1))
 
     table = exchange(adjoint)
     other = swap(table, "shots", 1)

time: 63.7 us -> 60.4 us (0.948)
  the two profiles are of different devices: /device:TPU:5 before, /device:TPU:1 now
where the time goes in v5:
time: 60.4 us; the launch traced here: 60.1 us
  blocking collectives  30.5 us (50%)
  starting transfers between devices  14.2 us (24%)
  Pallas kernels  11.9 us (20%)
  waiting for transfers between devices  2.64 us (4%)
  between operations  0.86 us (1%)
    all_to_all x2, blocking collectives, exchange(): lax.all_to_all(value, 'shots', 0, 0, axis_index_groups=lines, tiled=True)  30.5 us
    ppermute x4, starting transfers between devices, shift(): lax.ppermute(value, axes, [(i, (i + by) % count) for i in range(count)])  7.42 us
    ppermute x2, starting transfers between devices, swap(): return lax.ppermute(value, axes, [(i, i ^ bits) for i in range(count)])  6.81 us
    pallas_call x1, Pallas kernels, deposit_first(): pl.pallas_call(first_kernel, out_shape=(f32(8, 16, 512), jax.ShapeDtypeSt...  3.43 us
    pallas_call x1, Pallas kernels, pick_last(): pl.pallas_call(last_kernel, out_shape=f32(*cells.shape), in_specs=[VMEM]...  3.07 us
    ppermute x4, waiting for transfers between devices, shift(): lax.ppermute(value, axes, [(i, (i + by) % count) for i in range(count)])  2.63 us
    pallas_call x1, Pallas kernels, pick(): pl.pallas_call(pick_kernel, out_shape=(f32(table.shape[0], cells.shape[1]...  2.37 us
    pallas_call x1, Pallas kernels, deposit(): pl.pallas_call(functools.partial(deposit_kernel, 0), out_shape=f32(8, 16,...  2.34 us
  transfers between devices with their start and end apart: 6, of which 2 were waited for; matrix products, arithmetic and copies ran while one was open for 0% of the time, Pallas kernels for 8%

profile of v5, /device:TPU:1, one launch (start us, length us, event | category | flops | bytes accessed | tf_op | source)
XLA Modules:
  0.0 60.1 jit_solution(6413067881504973486)
XLA Ops:
  0.6 3.4 %deposit_first.1 = (f32[8,16,512]{2,1,0:T(8,128)S(1)}, s32[16,128]{1,0:T(8,128)S(1)}, s32[16,4096]{1,0:T(8,128)S(1)}, f32[16,4096]{1,0:T(8,128)S(1)}, f32[16,512]{1,0:T(8,128)S(1)}) custom-call(s32[16]{0:T(128)} %bitcast.6, f32[4]{0:T(128)} %refs_1_.1, s32[16,4096]{1,0:T(8,128)} %bitcast.4, f32[16,4096]{1,0:T(8,128)} %bitcast.5, s32[16,512]{1,0:T(8,128)} %refs_4_.1), custom_call_target="tpu_custom_call" | custom-call | flops 1073741824 | bytes 262144 | tf_op jit(solution)/shard_map/deposit_first/pallas_call | solution.py:107
  4.1 3.3 %collective-permute-start = (f32[8,16,512]{2,1,0:T(8,128)S(1)}, f32[8,16,512]{2,1,0:T(8,128)S(1)}, u32[]{:S(2)}, u32[]{:S(2)}) collective-permute-start(f32[8,16,512]{2,1,0:T(8,128)S(1)} %get-tuple-element.20), channel_id=1, source_target_pairs={{0,16},{16,0},{32,48},{48,32},{64,80},{80,64},{96,112},{112,96},{1... | collective-permute-start | bytes 786440 | tf_op jit(solution)/shard_map/ppermute | solution.py:307
  7.4 2.3 %deposit.1 = f32[8,16,512]{2,1,0:T(8,128)S(1)} custom-call(s32[16,128]{1,0:T(8,128)S(1)} %get-tuple-element.17.counts_ref, s32[16,4096]{1,0:T(8,128)S(1)} %get-tuple-element.18.cells_ref, f32[16,4096]{1,0:T(8,128)S(1)} %get-tuple-element.19.dose_ref), custom_call_target="tpu_custom_call" | custom-call | flops 1073741824 | bytes 262144 | tf_op jit(solution)/shard_map/deposit/pallas_call | solution.py:131
  9.7 0.0 collective-permute-done
  9.8 0.0 copy-start
  9.8 18.6 %all_to_all.10.parts_ref = f32[8,16,512]{2,1,0:T(8,128)S(1)} all-to-all(f32[8,16,512]{2,1,0:T(8,128)S(1)} %add.3), channel_id=1, replica_groups={{0,32,64,96,128,160,192,224},{16,48,80,112,144,176,208,240},{1,33,65,97..., dimensions={0} | all-to-all | bytes 524288 | tf_op jit(solution)/shard_map/all_to_all | solution.py:321
  28.4 0.0 copy-done
  28.4 0.1 gather.1
  28.5 1.3 %collective-permute-start.1 = (f32[16,128]{1,0:T(8,128)S(1)}, f32[16,128]{1,0:T(8,128)S(1)}, u32[]{:S(2)}, u32[]{:S(2)}) collective-permute-start(f32[16,128]{1,0:T(8,128)S(1)} %get-tuple-element.23), channel_id=1, source_target_pairs={{0,1},{1,2},{2,3},{3,0},{4,5},{5,6},{6,7},{7,4},{8,9},{9,10},{10,1... | collective-permute-start | bytes 24584 | tf_op jit(solution)/shard_map/ppermute | solution.py:312
  29.8 1.5 %collective-permute-start.2 = (f32[16,128]{1,0:T(8,128)S(1)}, f32[16,128]{1,0:T(8,128)S(1)}, u32[]{:S(2)}, u32[]{:S(2)}) collective-permute-start(f32[16,128]{1,0:T(8,128)S(1)} %get-tuple-element.24), channel_id=1, source_target_pairs={{0,3},{1,0},{2,1},{3,2},{4,7},{5,4},{6,5},{7,6},{8,11},{9,8},{10,9... | collective-permute-start | bytes 24584 | tf_op jit(solution)/shard_map/ppermute | solution.py:312
  31.3 1.0 %collective-permute-done.1.first_ref = f32[16,128]{1,0:T(8,128)S(1)} collective-permute-done((f32[16,128]{1,0:T(8,128)S(1)}, f32[16,128]{1,0:T(8,128)S(1)}, u32[]{:S(2)}, u32[]{:S(2)}) %collective-permute-start.1) | collective-permute-done | bytes 8224 | tf_op jit(solution)/shard_map/ppermute | solution.py:312
  32.3 0.0 collective-permute-done.2.second_ref
  32.3 0.1 widen.1
  32.4 1.4 %collective-permute-start.3 = (f32[16,640]{1,0:T(8,128)S(1)}, f32[16,640]{1,0:T(8,128)S(1)}, u32[]{:S(2)}, u32[]{:S(2)}) collective-permute-start(f32[16,640]{1,0:T(8,128)S(1)} %get-tuple-element.26), channel_id=1, source_target_pairs={{0,4},{4,8},{8,12},{12,16},{16,20},{20,24},{24,28},{28,32},{32,36}... | collective-permute-start | bytes 122888 | tf_op jit(solution)/shard_map/ppermute | solution.py:312
  33.8 3.3 %collective-permute-start.4 = (f32[16,640]{1,0:T(8,128)S(1)}, f32[16,640]{1,0:T(8,128)S(1)}, u32[]{:S(2)}, u32[]{:S(2)}) collective-permute-start(f32[16,640]{1,0:T(8,128)S(1)} %get-tuple-element.27), channel_id=1, source_target_pairs={{0,252},{4,0},{8,4},{12,8},{16,12},{20,16},{24,20},{28,24},{32,28}... | collective-permute-start | bytes 122888 | tf_op jit(solution)/shard_map/ppermute | solution.py:312
  37.1 1.6 %collective-permute-done.3.first_ref = f32[16,640]{1,0:T(8,128)S(1)} collective-permute-done((f32[16,640]{1,0:T(8,128)S(1)}, f32[16,640]{1,0:T(8,128)S(1)}, u32[]{:S(2)}, u32[]{:S(2)}) %collective-permute-start.3) | collective-permute-done | bytes 40992 | tf_op jit(solution)/shard_map/ppermute | solution.py:312
  38.7 0.0 collective-permute-done.4.second_ref
  38.7 0.5 blur.1
  39.2 11.8 %all_to_all.11.table_ref = f32[8,64,128]{2,1,0:T(8,128)S(1)} all-to-all(f32[8,64,128]{2,1,0:T(8,128)S(1)} %get-tuple-element.28), channel_id=1, replica_groups={{0,32,64,96,128,160,192,224},{16,48,80,112,144,176,208,240},{1,33,65,97..., dimensions={0} | all-to-all | bytes 524288 | tf_op jit(solution)/shard_map/all_to_all | solution.py:321
  51.0 3.5 %collective-permute-start.5 = (f32[8,64,128]{2,1,0:T(8,128)S(1)}, f32[8,64,128]{2,1,0:T(8,128)S(1)}, u32[]{:S(2)}, u32[]{:S(2)}) collective-permute-start(f32[8,64,128]{2,1,0:T(8,128)S(1)} %all_to_all.11.table_ref), channel_id=1, source_target_pairs={{0,16},{16,0},{32,48},{48,32},{64,80},{80,64},{96,112},{112,96},{1... | collective-permute-start | bytes 786440 | tf_op jit(solution)/shard_map/ppermute | solution.py:307
  54.5 2.4 %pick.1 = (f32[8,4096]{1,0:T(8,128)S(1)}, f32[16,512]{1,0:T(8,128)}) custom-call(s32[16,128]{1,0:T(8,128)S(1)} %get-tuple-element.17.counts_ref, s32[16,4096]{1,0:T(8,128)S(1)} %get-tuple-element.18.cells_ref, f32[8,64,128]{2,1,0:T(8,128)S(1)} %all_to_all.11.table_ref, f32[16,512]{1,0:T(8,128)S(1)} %get-tuple-element.29.blurred_ref), custom_call_target="tpu_custom_call" | custom-call | flops 1073741824 | bytes 262144 | tf_op jit(solution)/shard_map/pick/pallas_call | solution.py:250
  56.9 0.0 collective-permute-done.5.table_ref
  56.9 3.1 %pick_last.1 = f32[16,4096]{1,0:T(8,128)} custom-call(s32[16,128]{1,0:T(8,128)S(1)} %get-tuple-element.17.counts_ref, s32[16,4096]{1,0:T(8,128)S(1)} %get-tuple-element.18.cells_ref, f32[8,64,128]{2,1,0:T(8,128)S(1)} %collective-permute-done.5.table_ref, f32[8,4096]{1,0:T(8,128)S(1)} %get-tuple-element.31.own_ref), custom_call_target="tpu_custom_call" | custom-call | flops 1073741824 | bytes 262144 | tf_op jit(solution)/shard_map/pick_last/pallas_call | solution.py:289
  (1 shorter events, 0.0 us)
Async XLA Ops:
  4.1 5.7 %collective-permute-start = (f32[8,16,512]{2,1,0:T(8,128)S(1)}, f32[8,16,512]{2,1,0:T(8,128)S(1)}, u32[]{:S(2)}, u32[]{:S(2)}) collective-permute-start(f32[8,16,512]{2,1,0:T(8,128)S(1)} %get-tuple-element.20), channel_id=1, source_target_pairs={{0,16},{16,0},{32,48},{48,32},{64,80},{80,64},{96,112},{112,96},{1... | collective-permute-start | bytes 786440 | tf_op jit(solution)/shard_map/ppermute | solution.py:307
  9.8 18.6 %copy-start = (f32[16,512]{1,0:T(8,128)S(1)}, f32[16,512]{1,0:T(8,128)}, u32[]{:S(2)}) copy-start(f32[16,512]{1,0:T(8,128)} %target_ref.1) | copy-start | bytes 98308
  28.5 3.8 %collective-permute-start.1 = (f32[16,128]{1,0:T(8,128)S(1)}, f32[16,128]{1,0:T(8,128)S(1)}, u32[]{:S(2)}, u32[]{:S(2)}) collective-permute-start(f32[16,128]{1,0:T(8,128)S(1)} %get-tuple-element.23), channel_id=1, source_target_pairs={{0,1},{1,2},{2,3},{3,0},{4,5},{5,6},{6,7},{7,4},{8,9},{9,10},{10,1... | collective-permute-start | bytes 24584 | tf_op jit(solution)/shard_map/ppermute | solution.py:312
  29.8 2.5 %collective-permute-start.2 = (f32[16,128]{1,0:T(8,128)S(1)}, f32[16,128]{1,0:T(8,128)S(1)}, u32[]{:S(2)}, u32[]{:S(2)}) collective-permute-start(f32[16,128]{1,0:T(8,128)S(1)} %get-tuple-element.24), channel_id=1, source_target_pairs={{0,3},{1,0},{2,1},{3,2},{4,7},{5,4},{6,5},{7,6},{8,11},{9,8},{10,9... | collective-permute-start | bytes 24584 | tf_op jit(solution)/shard_map/ppermute | solution.py:312
  32.4 6.3 %collective-permute-start.3 = (f32[16,640]{1,0:T(8,128)S(1)}, f32[16,640]{1,0:T(8,128)S(1)}, u32[]{:S(2)}, u32[]{:S(2)}) collective-permute-start(f32[16,640]{1,0:T(8,128)S(1)} %get-tuple-element.26), channel_id=1, source_target_pairs={{0,4},{4,8},{8,12},{12,16},{16,20},{20,24},{24,28},{28,32},{32,36}... | collective-permute-start | bytes 122888 | tf_op jit(solution)/shard_map/ppermute | solution.py:312
  33.8 4.9 %collective-permute-start.4 = (f32[16,640]{1,0:T(8,128)S(1)}, f32[16,640]{1,0:T(8,128)S(1)}, u32[]{:S(2)}, u32[]{:S(2)}) collective-permute-start(f32[16,640]{1,0:T(8,128)S(1)} %get-tuple-element.27), channel_id=1, source_target_pairs={{0,252},{4,0},{8,4},{12,8},{16,12},{20,16},{24,20},{28,24},{32,28}... | collective-permute-start | bytes 122888 | tf_op jit(solution)/shard_map/ppermute | solution.py:312
  51.0 5.9 %collective-permute-start.5 = (f32[8,64,128]{2,1,0:T(8,128)S(1)}, f32[8,64,128]{2,1,0:T(8,128)S(1)}, u32[]{:S(2)}, u32[]{:S(2)}) collective-permute-start(f32[8,64,128]{2,1,0:T(8,128)S(1)} %all_to_all.11.table_ref), channel_id=1, source_target_pairs={{0,16},{16,0},{32,48},{48,32},{64,80},{80,64},{96,112},{112,96},{1... | collective-permute-start | bytes 786440 | tf_op jit(solution)/shard_map/ppermute | solution.py:307

commit v6 on v5

--- a/solution.py
+++ b/solution.py
@@ -139,43 +139,40 @@
     )(counts, cells, dose)
 
 
-def gather_kernel(parts_ref, spread_ref, target_ref, mid_ref, first_ref, second_ref):
+def gather_kernel(parts_ref, spread_ref, target_ref, mid_ref, down_ref, up_ref):
     strip = parts_ref[0]
     for z in range(1, parts_ref.shape[0]):
         strip = strip + parts_ref[z]
-    lane = lax.broadcasted_iota(jnp.int32, (16, LANES), 1)
-    left, right = jnp.zeros((16, LANES), F32), jnp.zeros((16, LANES), F32)
-    for i, value in enumerate((strip, spread_ref[...], target_ref[...])):
+    spread, target = spread_ref[...], target_ref[...]
+    for i, value in enumerate((strip, spread, target)):
         mid_ref[i] = value
+    line = lax.axis_index("shots") * lax.axis_size("gy") + lax.axis_index("gy")
+    last = lax.axis_size("shots") * lax.axis_size("gy") - 1
+    bottom = jnp.concatenate([strip[8:], spread[11:], target[13:]], axis=0)
+    top = jnp.concatenate([strip[:8], spread[:5], target[:3]], axis=0)
+    down_ref[...] = jnp.where(line == last, 0.0, bottom)
+    up_ref[...] = jnp.where(line == 0, 0.0, top)
+
+
+def heighten_kernel(mid_ref, above_ref, below_ref, tall_ref, right_ref, left_ref):
+    above, below = above_ref[...], below_ref[...]
+    blank = lambda rows: jnp.zeros((rows, above.shape[1]), F32)
+    fields = (
+        [above[:8], mid_ref[0], below[:8]],
+        [blank(3), above[8:13], mid_ref[1], below[8:13], blank(3)],
+        [blank(5), above[13:], mid_ref[2], below[13:], blank(5)],
+    )
+    lane = lax.broadcasted_iota(jnp.int32, (32, LANES), 1)
+    left, right = jnp.zeros((32, LANES), F32), jnp.zeros((32, LANES), F32)
+    for i, pieces in enumerate(fields):
+        value = jnp.concatenate(pieces, axis=0)
+        tall_ref[i] = value
         here = (lane >= 16 * i) & (lane < 16 * i + 8)
         left = jnp.where(here, pltpu.roll(value[:, :LANES], 16 * i, 1), left)
         right = jnp.where(here, pltpu.roll(value[:, -LANES:], 16 * i + 8, 1), right)
     column, columns = lax.axis_index("gx"), lax.axis_size("gx")
-    first_ref[...] = jnp.where(column == columns - 1, 0.0, right)
-    second_ref[...] = jnp.where(column == 0, 0.0, left)
-
-
-def widen_kernel(mid_ref, first_ref, second_ref, wide_ref, send_ref, later_ref):
-    near = lax.broadcasted_iota(jnp.int32, (16, LANES), 1) < LANES // 2
-    left, right = first_ref[...], second_ref[...]
-    for i in range(3):
-        tile = jnp.where(
-            near,
-            pltpu.roll(right, (LANES - 16 * i) % LANES, 1),
-            pltpu.roll(left, LANES - 8 - 16 * i, 1),
-        )
-        wide = jnp.concatenate([mid_ref[i], tile], axis=1)
-        wide_ref[i] = wide
-        if i == 0:
-            top, bottom = wide[:8], wide[8:]
-        elif i == 1:
-            top, bottom = jnp.concatenate([top, wide[:5]]), jnp.concatenate([bottom, wide[11:]])
-        else:
-            top, bottom = jnp.concatenate([top, wide[:3]]), jnp.concatenate([bottom, wide[13:]])
-    line = lax.axis_index("shots") * lax.axis_size("gy") + lax.axis_index("gy")
-    last = lax.axis_size("shots") * lax.axis_size("gy") - 1
-    send_ref[...] = jnp.where(line == last, 0.0, bottom)
-    later_ref[...] = jnp.where(line == 0, 0.0, top)
+    right_ref[...] = jnp.where(column == columns - 1, 0.0, right)
+    left_ref[...] = jnp.where(column == 0, 0.0, left)
 
 
 def neighbours(field):
@@ -188,17 +185,18 @@
     )
 
 
-def blur_kernel(wide_ref, first_ref, second_ref, exposure_ref, adjoint_ref):
-    above, below = first_ref[...], second_ref[...]
-    width = wide_ref.shape[2]
-    blank = lambda rows: jnp.zeros((rows, width), F32)
-    field = jnp.concatenate([above[:8], wide_ref[0], below[:8]], axis=0)
-    spread = jnp.concatenate(
-        [blank(3), above[8:13], wide_ref[1], below[8:13], blank(3)], axis=0
-    )
-    target = jnp.concatenate(
-        [blank(5), above[13:], wide_ref[2], below[13:], blank(5)], axis=0
-    )
+def blur_kernel(tall_ref, left_ref, right_ref, exposure_ref, adjoint_ref):
+    left, right = left_ref[...], right_ref[...]
+    near = lax.broadcasted_iota(jnp.int32, (32, LANES), 1) < LANES // 2
+    fields = []
+    for i in range(3):
+        tile = jnp.where(
+            near,
+            pltpu.roll(right, (LANES - 16 * i) % LANES, 1),
+            pltpu.roll(left, LANES - 8 - 16 * i, 1),
+        )
+        fields.append(jnp.concatenate([tall_ref[i], tile], axis=1))
+    field, spread, target = fields
     for step in range(STEPS):
         field = field + spread * (neighbours(field) - 4.0 * field)
     exposure_ref[...] = field[8:24, :-LANES]
@@ -326,23 +324,24 @@
     away = swap(away, "shots", 1)
     parts = exchange(deposit(counts, cells, dose) + away)
 
-    mid, first, second = pl.pallas_call(
+    row, edge = f32(16, 512), f32(32, LANES)
+    mid, down, up = pl.pallas_call(
         gather_kernel,
-        out_shape=(f32(3, 16, 512), f32(16, LANES), f32(16, LANES)),
+        out_shape=(f32(3, 16, 512), row, row),
         in_specs=[VMEM] * 3,
         out_specs=(VMEM,) * 3,
         compiler_params=PARAMS,
         name="gather",
     )(parts, spread, target)
-    wide, first, second = pl.pallas_call(
-        widen_kernel,
-        out_shape=(f32(3, 16, 640), f32(16, 640), f32(16, 640)),
+    rows = ("shots", "gy")
+    tall, right, left = pl.pallas_call(
+        heighten_kernel,
+        out_shape=(f32(3, 32, 512), edge, edge),
         in_specs=[VMEM] * 3,
         out_specs=(VMEM,) * 3,
         compiler_params=PARAMS,
-        name="widen",
-    )(mid, shift(first, "gx", 1), shift(second, "gx", -1))
-    rows = ("shots", "gy")
+        name="heighten",
+    )(mid, shift(down, rows, 1), shift(up, rows, -1))
     blurred, adjoint = pl.pallas_call(
         blur_kernel,
         out_shape=(f32(16, 512), f32(shots // 2, 64, LANES)),
@@ -350,7 +349,7 @@
         out_specs=(VMEM,) * 2,
         compiler_params=PARAMS,
         name="blur",
-    )(wide, shift(first, rows, 1), shift(second, rows, -1))
+    )(tall, shift(right, "gx", 1), shift(left, "gx", -1))
 
     table = exchange(adjoint)
     other = swap(table, "shots", 1)

time: 60.4 us -> 60.4 us (level)
    ppermute x4, starting transfers between devices: 7.42 us -> 6.01 us  [shift(): lax.ppermute(value, axes, [(i, (i + by) % count) for i in range(count)])]
    ppermute x2, starting transfers between devices: 6.81 us -> 8.19 us  [swap(): return lax.ppermute(value, axes, [(i, i ^ bits) for i in range(count)])]
where the time goes in v6:
time: 60.4 us; the launch traced here: 60.2 us
  blocking collectives  30.5 us (50%)
  starting transfers between devices  14.2 us (24%)
  Pallas kernels  12 us (20%)
  waiting for transfers between devices  2.64 us (4%)
  between operations  0.87 us (1%)
    all_to_all x2, blocking collectives, exchange(): lax.all_to_all(value, 'shots', 0, 0, axis_index_groups=lines, tiled=True)  30.5 us
    ppermute x2, starting transfers between devices, swap(): return lax.ppermute(value, axes, [(i, i ^ bits) for i in range(count)])  8.19 us
    ppermute x4, starting transfers between devices, shift(): lax.ppermute(value, axes, [(i, (i + by) % count) for i in range(count)])  6.01 us
    pallas_call x1, Pallas kernels, deposit_first(): pl.pallas_call(first_kernel, out_shape=(f32(8, 16, 512), jax.ShapeDtypeSt...  3.43 us
    pallas_call x1, Pallas kernels, pick_last(): pl.pallas_call(last_kernel, out_shape=f32(*cells.shape), in_specs=[VMEM]...  3.07 us
    ppermute x4, waiting for transfers between devices, shift(): lax.ppermute(value, axes, [(i, (i + by) % count) for i in range(count)])  2.64 us
    pallas_call x1, Pallas kernels, pick(): pl.pallas_call(pick_kernel, out_shape=(f32(table.shape[0], cells.shape[1]...  2.37 us
    pallas_call x1, Pallas kernels, deposit(): pl.pallas_call(functools.partial(deposit_kernel, 0), out_shape=f32(8, 16,...  2.34 us
  transfers between devices with their start and end apart: 6, of which 2 were waited for; matrix products, arithmetic and copies ran while one was open for 0% of the time, Pallas kernels for 8%

profile of v6, /device:TPU:1, one launch (start us, length us, event | category | flops | bytes accessed | tf_op | source)
XLA Modules:
  0.0 60.2 jit_solution(2534651826436205430)
XLA Ops:
  0.6 3.4 %deposit_first.1 = (f32[8,16,512]{2,1,0:T(8,128)S(1)}, s32[16,128]{1,0:T(8,128)S(1)}, s32[16,4096]{1,0:T(8,128)S(1)}, f32[16,4096]{1,0:T(8,128)S(1)}, f32[16,512]{1,0:T(8,128)S(1)}) custom-call(s32[16]{0:T(128)} %bitcast.6, f32[4]{0:T(128)} %refs_1_.1, s32[16,4096]{1,0:T(8,128)} %bitcast.4, f32[16,4096]{1,0:T(8,128)} %bitcast.5, s32[16,512]{1,0:T(8,128)} %refs_4_.1), custom_call_target="tpu_custom_call" | custom-call | flops 1073741824 | bytes 262144 | tf_op jit(solution)/shard_map/deposit_first/pallas_call | solution.py:107
  4.1 3.3 %collective-permute-start = (f32[8,16,512]{2,1,0:T(8,128)S(1)}, f32[8,16,512]{2,1,0:T(8,128)S(1)}, u32[]{:S(2)}, u32[]{:S(2)}) collective-permute-start(f32[8,16,512]{2,1,0:T(8,128)S(1)} %get-tuple-element.20), channel_id=1, source_target_pairs={{0,16},{16,0},{32,48},{48,32},{64,80},{80,64},{96,112},{112,96},{1... | collective-permute-start | bytes 786440 | tf_op jit(solution)/shard_map/ppermute | solution.py:305
  7.4 2.3 %deposit.1 = f32[8,16,512]{2,1,0:T(8,128)S(1)} custom-call(s32[16,128]{1,0:T(8,128)S(1)} %get-tuple-element.17.counts_ref, s32[16,4096]{1,0:T(8,128)S(1)} %get-tuple-element.18.cells_ref, f32[16,4096]{1,0:T(8,128)S(1)} %get-tuple-element.19.dose_ref), custom_call_target="tpu_custom_call" | custom-call | flops 1073741824 | bytes 262144 | tf_op jit(solution)/shard_map/deposit/pallas_call | solution.py:131
  9.7 0.0 collective-permute-done
  9.8 0.0 copy-start
  9.8 18.6 %all_to_all.10.parts_ref = f32[8,16,512]{2,1,0:T(8,128)S(1)} all-to-all(f32[8,16,512]{2,1,0:T(8,128)S(1)} %add.3), channel_id=1, replica_groups={{0,32,64,96,128,160,192,224},{16,48,80,112,144,176,208,240},{1,33,65,97..., dimensions={0} | all-to-all | bytes 524288 | tf_op jit(solution)/shard_map/all_to_all | solution.py:319
  28.4 0.0 copy-done
  28.5 1.4 %collective-permute-start.1 = (f32[16,512]{1,0:T(8,128)S(1)}, f32[16,512]{1,0:T(8,128)S(1)}, u32[]{:S(2)}, u32[]{:S(2)}) collective-permute-start(f32[16,512]{1,0:T(8,128)S(1)} %get-tuple-element.23), channel_id=1, source_target_pairs={{0,4},{4,8},{8,12},{12,16},{16,20},{20,24},{24,28},{28,32},{32,36}... | collective-permute-start | bytes 98312 | tf_op jit(solution)/shard_map/ppermute | solution.py:310
  29.8 1.9 %collective-permute-start.2 = (f32[16,512]{1,0:T(8,128)S(1)}, f32[16,512]{1,0:T(8,128)S(1)}, u32[]{:S(2)}, u32[]{:S(2)}) collective-permute-start(f32[16,512]{1,0:T(8,128)S(1)} %get-tuple-element.24), channel_id=1, source_target_pairs={{0,252},{4,0},{8,4},{12,8},{16,12},{20,16},{24,20},{28,24},{32,28}... | collective-permute-start | bytes 98312 | tf_op jit(solution)/shard_map/ppermute | solution.py:310
  31.7 1.5 %collective-permute-done.1.above_ref = f32[16,512]{1,0:T(8,128)S(1)} collective-permute-done((f32[16,512]{1,0:T(8,128)S(1)}, f32[16,512]{1,0:T(8,128)S(1)}, u32[]{:S(2)}, u32[]{:S(2)}) %collective-permute-start.1) | collective-permute-done | bytes 32800 | tf_op jit(solution)/shard_map/ppermute | solution.py:310
  33.2 0.0 collective-permute-done.2.below_ref
  33.2 0.1 heighten.1
  33.3 1.3 %collective-permute-start.3 = (f32[32,128]{1,0:T(8,128)S(1)}, f32[32,128]{1,0:T(8,128)S(1)}, u32[]{:S(2)}, u32[]{:S(2)}) collective-permute-start(f32[32,128]{1,0:T(8,128)S(1)} %get-tuple-element.26), channel_id=1, source_target_pairs={{0,1},{1,2},{2,3},{3,0},{4,5},{5,6},{6,7},{7,4},{8,9},{9,10},{10,1... | collective-permute-start | bytes 49160 | tf_op jit(solution)/shard_map/ppermute | solution.py:310
  34.6 1.5 %collective-permute-start.4 = (f32[32,128]{1,0:T(8,128)S(1)}, f32[32,128]{1,0:T(8,128)S(1)}, u32[]{:S(2)}, u32[]{:S(2)}) collective-permute-start(f32[32,128]{1,0:T(8,128)S(1)} %get-tuple-element.27), channel_id=1, source_target_pairs={{0,3},{1,0},{2,1},{3,2},{4,7},{5,4},{6,5},{7,6},{8,11},{9,8},{10,9... | collective-permute-start | bytes 49160 | tf_op jit(solution)/shard_map/ppermute | solution.py:310
  36.1 1.1 %collective-permute-done.3.left_ref = f32[32,128]{1,0:T(8,128)S(1)} collective-permute-done((f32[32,128]{1,0:T(8,128)S(1)}, f32[32,128]{1,0:T(8,128)S(1)}, u32[]{:S(2)}, u32[]{:S(2)}) %collective-permute-start.3) | collective-permute-done | bytes 16416 | tf_op jit(solution)/shard_map/ppermute | solution.py:310
  37.2 0.0 collective-permute-done.4.right_ref
  37.2 0.6 %blur.1 = (f32[16,512]{1,0:T(8,128)S(1)}, f32[8,64,128]{2,1,0:T(8,128)S(1)}) custom-call(f32[3,32,512]{2,1,0:T(8,128)S(1)} %get-tuple-element.25.tall_ref, f32[32,128]{1,0:T(8,128)S(1)} %collective-permute-done.3.left_ref, f32[32,128]{1,0:T(8,128)S(1)} %collective-permute-done.4.right_ref), custom_call_target="tpu_custom_call" | custom-call | tf_op jit(solution)/shard_map/blur/pallas_call | solution.py:345
  37.8 11.9 %all_to_all.11.table_ref = f32[8,64,128]{2,1,0:T(8,128)S(1)} all-to-all(f32[8,64,128]{2,1,0:T(8,128)S(1)} %get-tuple-element.28), channel_id=1, replica_groups={{0,32,64,96,128,160,192,224},{16,48,80,112,144,176,208,240},{1,33,65,97..., dimensions={0} | all-to-all | bytes 524288 | tf_op jit(solution)/shard_map/all_to_all | solution.py:319
  49.7 4.9 %collective-permute-start.5 = (f32[8,64,128]{2,1,0:T(8,128)S(1)}, f32[8,64,128]{2,1,0:T(8,128)S(1)}, u32[]{:S(2)}, u32[]{:S(2)}) collective-permute-start(f32[8,64,128]{2,1,0:T(8,128)S(1)} %all_to_all.11.table_ref), channel_id=1, source_target_pairs={{0,16},{16,0},{32,48},{48,32},{64,80},{80,64},{96,112},{112,96},{1... | collective-permute-start | bytes 786440 | tf_op jit(solution)/shard_map/ppermute | solution.py:305
  54.6 2.4 %pick.1 = (f32[8,4096]{1,0:T(8,128)S(1)}, f32[16,512]{1,0:T(8,128)}) custom-call(s32[16,128]{1,0:T(8,128)S(1)} %get-tuple-element.17.counts_ref, s32[16,4096]{1,0:T(8,128)S(1)} %get-tuple-element.18.cells_ref, f32[8,64,128]{2,1,0:T(8,128)S(1)} %all_to_all.11.table_ref, f32[16,512]{1,0:T(8,128)S(1)} %get-tuple-element.29.blurred_ref), custom_call_target="tpu_custom_call" | custom-call | flops 1073741824 | bytes 262144 | tf_op jit(solution)/shard_map/pick/pallas_call | solution.py:248
  57.0 0.0 collective-permute-done.5.table_ref
  57.0 3.1 %pick_last.1 = f32[16,4096]{1,0:T(8,128)} custom-call(s32[16,128]{1,0:T(8,128)S(1)} %get-tuple-element.17.counts_ref, s32[16,4096]{1,0:T(8,128)S(1)} %get-tuple-element.18.cells_ref, f32[8,64,128]{2,1,0:T(8,128)S(1)} %collective-permute-done.5.table_ref, f32[8,4096]{1,0:T(8,128)S(1)} %get-tuple-element.31.own_ref), custom_call_target="tpu_custom_call" | custom-call | flops 1073741824 | bytes 262144 | tf_op jit(solution)/shard_map/pick_last/pallas_call | solution.py:287
  (2 shorter events, 0.1 us)
Async XLA Ops:
  4.1 5.7 %collective-permute-start = (f32[8,16,512]{2,1,0:T(8,128)S(1)}, f32[8,16,512]{2,1,0:T(8,128)S(1)}, u32[]{:S(2)}, u32[]{:S(2)}) collective-permute-start(f32[8,16,512]{2,1,0:T(8,128)S(1)} %get-tuple-element.20), channel_id=1, source_target_pairs={{0,16},{16,0},{32,48},{48,32},{64,80},{80,64},{96,112},{112,96},{1... | collective-permute-start | bytes 786440 | tf_op jit(solution)/shard_map/ppermute | solution.py:305
  9.8 18.6 %copy-start = (f32[16,512]{1,0:T(8,128)S(1)}, f32[16,512]{1,0:T(8,128)}, u32[]{:S(2)}) copy-start(f32[16,512]{1,0:T(8,128)} %target_ref.1) | copy-start | bytes 98308
  28.5 4.8 %collective-permute-start.1 = (f32[16,512]{1,0:T(8,128)S(1)}, f32[16,512]{1,0:T(8,128)S(1)}, u32[]{:S(2)}, u32[]{:S(2)}) collective-permute-start(f32[16,512]{1,0:T(8,128)S(1)} %get-tuple-element.23), channel_id=1, source_target_pairs={{0,4},{4,8},{8,12},{12,16},{16,20},{20,24},{24,28},{28,32},{32,36}... | collective-permute-start | bytes 98312 | tf_op jit(solution)/shard_map/ppermute | solution.py:310
  29.8 3.4 %collective-permute-start.2 = (f32[16,512]{1,0:T(8,128)S(1)}, f32[16,512]{1,0:T(8,128)S(1)}, u32[]{:S(2)}, u32[]{:S(2)}) collective-permute-start(f32[16,512]{1,0:T(8,128)S(1)} %get-tuple-element.24), channel_id=1, source_target_pairs={{0,252},{4,0},{8,4},{12,8},{16,12},{20,16},{24,20},{28,24},{32,28}... | collective-permute-start | bytes 98312 | tf_op jit(solution)/shard_map/ppermute | solution.py:310
  33.3 3.9 %collective-permute-start.3 = (f32[32,128]{1,0:T(8,128)S(1)}, f32[32,128]{1,0:T(8,128)S(1)}, u32[]{:S(2)}, u32[]{:S(2)}) collective-permute-start(f32[32,128]{1,0:T(8,128)S(1)} %get-tuple-element.26), channel_id=1, source_target_pairs={{0,1},{1,2},{2,3},{3,0},{4,5},{5,6},{6,7},{7,4},{8,9},{9,10},{10,1... | collective-permute-start | bytes 49160 | tf_op jit(solution)/shard_map/ppermute | solution.py:310
  34.6 2.6 %collective-permute-start.4 = (f32[32,128]{1,0:T(8,128)S(1)}, f32[32,128]{1,0:T(8,128)S(1)}, u32[]{:S(2)}, u32[]{:S(2)}) collective-permute-start(f32[32,128]{1,0:T(8,128)S(1)} %get-tuple-element.27), channel_id=1, source_target_pairs={{0,3},{1,0},{2,1},{3,2},{4,7},{5,4},{6,5},{7,6},{8,11},{9,8},{10,9... | collective-permute-start | bytes 49160 | tf_op jit(solution)/shard_map/ppermute | solution.py:310
  49.7 7.3 %collective-permute-start.5 = (f32[8,64,128]{2,1,0:T(8,128)S(1)}, f32[8,64,128]{2,1,0:T(8,128)S(1)}, u32[]{:S(2)}, u32[]{:S(2)}) collective-permute-start(f32[8,64,128]{2,1,0:T(8,128)S(1)} %all_to_all.11.table_ref), channel_id=1, source_target_pairs={{0,16},{16,0},{32,48},{48,32},{64,80},{80,64},{96,112},{112,96},{1... | collective-permute-start | bytes 786440 | tf_op jit(solution)/shard_map/ppermute | solution.py:305
